TPU v7x, 32 devices: a whole 2x2x4 slice. The times are simulated.
32 devices in a mesh: grp: 4 (over x, core), ep: 8 (over z, y).
Axes of the slice: x: 2, y: 2, z: 4, core: 2. Of those that a mesh axis runs over, the one named last changes fastest.
Arguments:
- tokens: bfloat16 [4, 32, 5120], P('grp', 'ep'), may hold values from -6 to 6
- cotangent: bfloat16 [4, 32, 5120], P('grp', 'ep'), may hold values from -1.5 to 1.5
- counts: int32 [4, 8, 1], P('grp', 'ep'), may hold values from 0 to 4, as said below
- destination: int32 [4, 8, 4], P('grp', 'ep'), may hold values from 0 to 3, each once within a row
- placement: int32 [8], replicated, may hold values from 0 to 7, each once
- gate_up_weight: bfloat16 [8, 2, 5120, 128], P('ep', None, 'grp'), may hold values from -0.078125 to 0.078125
- down_weight: bfloat16 [8, 5120, 128], P('ep', 'grp'), may hold values from -0.1875 to 0.1875
Outputs:
- layer_out: bfloat16 [4, 32, 5120], P('grp', 'ep')
- input_grad: bfloat16 [4, 32, 5120], P('grp', 'ep')
- gate_up_grad: float32 [8, 2, 5120, 128], P('ep', None, 'grp')
- down_grad: float32 [8, 5120, 128], P('ep', 'grp')
Inputs may be any that keep to these rules, and one draw needn't show every extreme that they name: counts[g, j, e] is the number of kept slots of expert e on device (g, j) after reassignment; some device has all 4 slots of an expert kept in every draw. `destination`: the 4 blocks of one device go to 4 different groups. `placement`: each expert slice is served by exactly one owner.
All inputs are finite; a program needn't handle non-finite values.
Results may differ from a plain program's by a relative error of at most 0.017.
Values may be sent and summed in bfloat16 or wider, within the bound.
A program may use at most 64 MiB of HBM per device.

v0:
```python
import jax
import jax.numpy as jnp
from jax import lax
from jax.sharding import PartitionSpec as P


def swiglu_backward(gate_up, hidden_grad):
    gate_part = gate_up[0]
    up_part = gate_up[1]
    sigmoid_gate = jax.nn.sigmoid(gate_part)
    activated = gate_part * sigmoid_gate
    hidden = (activated * up_part).astype(jnp.bfloat16)
    gate_grad = hidden_grad * up_part * sigmoid_gate * (1.0 + gate_part * (1.0 - sigmoid_gate))
    up_grad = hidden_grad * activated
    return (hidden, jnp.stack([gate_grad, up_grad]).astype(jnp.bfloat16))


def body(tokens, cotangent, counts, destination, placement, gate_up_weight, down_weight):
    groups = lax.axis_size("grp")
    owners = lax.axis_size("ep")
    tok_dev = tokens.shape[1]
    model_width = tokens.shape[2]
    experts = counts.shape[2]
    capacity = tok_dev // experts
    block_rows = tok_dev // groups
    split_count = owners // experts
    row_count = owners * capacity
    order = jnp.argsort(destination[0, 0])
    send_tokens = jnp.take(tokens[0].reshape(groups, block_rows, model_width), order, axis=0)
    send_cotangent = jnp.take(cotangent[0].reshape(groups, block_rows, model_width), order, axis=0)
    here_tokens, here_cotangent = (
        lax.all_to_all(send_tokens, "grp", split_axis=0, concat_axis=0, tiled=True),
        lax.all_to_all(send_cotangent, "grp", split_axis=0, concat_axis=0, tiled=True),
    )
    slot_ids = lax.broadcasted_iota(jnp.int32, (experts, capacity), 1)
    keep = (slot_ids < counts[0, 0][:, None])[:, :, None]
    nothing = jnp.zeros((), jnp.bfloat16)
    kept_tokens = jnp.where(keep, here_tokens.reshape(experts, capacity, model_width), nothing)
    kept_cotangent = jnp.where(
        keep, here_cotangent.reshape(experts, capacity, model_width), nothing
    )
    expert_of = placement // split_count
    routed_tokens, routed_cotangent = (
        lax.all_to_all(
            jnp.take(kept_tokens, expert_of, axis=0), "ep", split_axis=0, concat_axis=0, tiled=True
        ),
        lax.all_to_all(
            jnp.take(kept_cotangent, expert_of, axis=0),
            "ep",
            split_axis=0,
            concat_axis=0,
            tiled=True,
        ),
    )
    routed_tokens = routed_tokens.reshape(row_count, model_width)
    routed_cotangent = routed_cotangent.reshape(row_count, model_width)
    stacked_down = down_weight[:, None]
    full_gate_up, full_down = (
        lax.all_gather(gate_up_weight, "grp", axis=2, tiled=True),
        lax.all_gather(stacked_down, "grp", axis=2, tiled=True),
    )
    full_gate_up = full_gate_up[0]
    full_down = full_down[0, 0]
    gate_up = jnp.einsum(
        "rd,kds->krs", routed_tokens, full_gate_up, preferred_element_type=jnp.float32
    )
    hidden_grad = jnp.dot(routed_cotangent, full_down, preferred_element_type=jnp.float32)
    hidden, grad_rows = swiglu_backward(gate_up, hidden_grad)
    forward_part = (
        jnp.einsum("rs,ds->rd", hidden, full_down, preferred_element_type=jnp.float32)
        .astype(jnp.bfloat16)
        .reshape(owners, capacity, model_width)
    )
    backward_part = (
        jnp.einsum("krs,kds->rd", grad_rows, full_gate_up, preferred_element_type=jnp.float32)
        .astype(jnp.bfloat16)
        .reshape(owners, capacity, model_width)
    )
    owner_table = (
        expert_of[:, None] == lax.broadcasted_iota(jnp.int32, (owners, experts), 1)
    ).astype(jnp.bfloat16)

    def combine(returned):
        summed = jnp.einsum(
            "jcd,je->ecd", returned, owner_table, preferred_element_type=jnp.float32
        )
        return summed.astype(jnp.bfloat16).reshape(1, tok_dev, model_width)

    layer_out = combine(lax.all_to_all(forward_part, "ep", split_axis=0, concat_axis=0, tiled=True))
    input_grad = combine(
        lax.all_to_all(backward_part, "ep", split_axis=0, concat_axis=0, tiled=True)
    )
    gate_up_term = jnp.einsum(
        "rd,krs->kds", routed_tokens, grad_rows, preferred_element_type=jnp.float32
    )
    down_term = jnp.einsum(
        "rd,rs->ds", routed_cotangent, hidden, preferred_element_type=jnp.float32
    )
    gate_up_grad, down_grad = (
        lax.psum_scatter(
            gate_up_term[None].astype(jnp.bfloat16), "grp", scatter_dimension=2, tiled=True
        ).astype(jnp.float32),
        lax.psum_scatter(
            down_term[None, None].astype(jnp.bfloat16), "grp", scatter_dimension=2, tiled=True
        ).astype(jnp.float32),
    )
    return (layer_out, input_grad, gate_up_grad, down_grad[:, 0])


def solution(mesh):
    return jax.shard_map(
        body,
        mesh=mesh,
        in_specs=(
            P("grp", "ep", None),
            P("grp", "ep", None),
            P("grp", "ep", None),
            P("grp", "ep", None),
            P(),
            P("ep", None, "grp", None),
            P("ep", "grp", None),
        ),
        out_specs=(
            P("grp", "ep", None),
            P("grp", "ep", None),
            P("ep", None, "grp", None),
            P("ep", "grp", None),
        ),
        check_vma=False,
    )
```

profile of v0, /device:TPU:0, one launch (start us, length us, event | category | flops | bytes accessed | tf_op | source)
XLA Modules:
  0.0 135.7 jit_solution(14142553181255238331)
XLA Ops:
  7.2 0.0 all-gather.4.cloned.1.call-start
  7.2 0.7 all-gather.4.cloned.1.call-update
  7.9 1.4 %sort.17 = (s32[4]{0:T(128)}, s32[4]{0:T(128)S(1)}) sort(s32[4]{0:T(128)} %bitcast.125, s32[4]{0:T(128)S(1)} %iota.12), dimensions={0}, to_apply=%region_0.0 | sort | flops 8 | bytes 64 | tf_op jit(solution)/shard_map/jit(argsort)/sort | solution.py:28
  9.3 0.6 gather_fusion.1
  9.9 1.4 %gather_fusion = bf16[4,5120]{1,0:T(4,128)(2,1)S(1)} fusion(bf16[4,5120]{1,0:T(4,128)(2,1)} %bitcast.124, s32[1024]{0:T(1024)S(1)} %pad_clamp_fusion), kind=kCustom, calls=%fused_computation.clone | custom fusion | bytes 81936 | tf_op jit(solution)/shard_map/jit(_take)/gather | solution.py:29
  11.4 0.1 bitcast_select_fusion.2
  11.5 0.5 broadcast.187
  12.0 0.7 reduce.1
  12.7 0.6 reshape.197
  13.3 4.2 %all-to-all-start = ((bf16[4,2,2560]{2,1,0:T(2,128)(2,1)}), bf16[4,2,2560]{2,1,0:T(2,128)(2,1)S(1)}, u32[]{:S(2)}, u32[]{:S(2)}) async-start(bf16[4,2,2560]{2,1,0:T(2,128)(2,1)} %reshape.197), calls=%async_computation | async-start | bytes 81920 | tf_op jit(solution)/shard_map/all_to_all | solution.py:32
  17.6 0.7 all-gather.6.cloned.1.call-update
  18.3 0.7 compare_and_fusion
  19.6 0.7 reduce
  20.3 0.6 reshape.199
  20.9 0.6 all-to-all-done
  21.5 3.3 %all-to-all-start.3 = ((bf16[4,2,2560]{2,1,0:T(2,128)(2,1)}), bf16[4,2,2560]{2,1,0:T(2,128)(2,1)S(1)}, u32[]{:S(2)}, u32[]{:S(2)}) async-start(bf16[4,2,2560]{2,1,0:T(2,128)(2,1)} %reshape.199), calls=%async_computation.3 | async-start | bytes 81920 | tf_op jit(solution)/shard_map/all_to_all | solution.py:33
  24.9 4.3 %all-to-all-done.3 = bf16[4,2,2560]{2,1,0:T(2,128)(2,1)S(1)} async-done(((bf16[4,2,2560]{2,1,0:T(2,128)(2,1)}), bf16[4,2,2560]{2,1,0:T(2,128)(2,1)S(1)}, u32[]{:S(2)}, u32[]{:S(2)}) %all-to-all-start.3) | async-done | bytes 40992 | tf_op jit(solution)/shard_map/all_to_all | solution.py:33
  29.2 0.1 fusion.18
  29.4 1.0 broadcast_select_fusion
  30.4 17.1 %all_to_all.30 = bf16[8,4,5120]{2,1,0:T(4,128)(2,1)S(1)} all-to-all(bf16[8,4,5120]{2,1,0:T(4,128)(2,1)S(1)} %get-tuple-element.22), channel_id=1, replica_groups=mesh['grp'=4,'ep'=8] {'ep'}, dimensions={0} | all-to-all | bytes 655360 | tf_op jit(solution)/shard_map/all_to_all | solution.py:47
  47.5 3.4 %all-to-all-start.1 = ((bf16[8,4,5120]{2,1,0:T(4,128)(2,1)}), bf16[8,4,5120]{2,1,0:T(4,128)(2,1)S(1)}, u32[]{:S(2)}, u32[]{:S(2)}) async-start(bf16[8,4,5120]{2,1,0:T(4,128)(2,1)} %get-tuple-element.23), calls=%async_computation.1 | async-start | bytes 655360 | tf_op jit(solution)/shard_map/all_to_all | solution.py:44
  51.0 0.0 reduce-scatter.5.cloned.1.call-start
  51.0 0.1 reshape.151
  51.1 9.6 %all-to-all-done.1 = bf16[8,4,5120]{2,1,0:T(4,128)(2,1)S(1)} async-done(((bf16[8,4,5120]{2,1,0:T(4,128)(2,1)}), bf16[8,4,5120]{2,1,0:T(4,128)(2,1)S(1)}, u32[]{:S(2)}, u32[]{:S(2)}) %all-to-all-start.1) | async-done | bytes 327712 | tf_op jit(solution)/shard_map/all_to_all | solution.py:44
  60.6 0.1 reshape.190
  60.7 0.0 all-gather.4.cloned.1.call-done
  60.7 2.3 %fusion.9 = f32[2,32,128]{2,1,0:T(8,128)S(1)} fusion(bf16[32,5120,1]{1,0,2:T(8,128)(2,1)S(1)} %reshape.190, bf16[1,2,5120,128]{3,2,1,0:T(8,128)(2,1)} %all-gather.4.cloned.1.call-done), kind=kOutput, calls=%fused_computation.15 | convolution fusion | flops 83886080 | bytes 2981888 | tf_op jit(solution)/shard_map/rd,kds->krs/dot_general | solution.py:64
  63.1 1.6 %fusion.1 = bf16[1,1,5120,128]{3,2,1,0:T(8,128)(2,1)} fusion(bf16[32,5120]{1,0:T(8,128)(2,1)S(1)} %reshape.151, bf16[1,32,128]{2,1,0:T(8,128)(2,1)S(1)} %multiply_convert_fusion), kind=kOutput, calls=%fused_computation.5 | convolution fusion | flops 42598400 | bytes 1646592 | tf_op jit(solution)/shard_map/rd,rs->ds/dot_general | solution.py:96
  64.7 0.0 reduce-scatter.5.cloned.1.call-update
  64.7 0.0 reduce-scatter.3.cloned.1.call-start
  64.8 0.0 all-gather.6.cloned.1.call-done
  64.8 1.7 %fusion.32 = (bf16[1,32,128]{2,1,0:T(8,128)(2,1)S(1)}, bf16[1,32,128]{2,1,0:T(8,128)(2,1)S(1)}) fusion(f32[2,32,128]{2,1,0:T(8,128)S(1)} %fusion.9, bf16[32,5120]{1,0:T(8,128)(2,1)S(1)} %reshape.151, bf16[1,5120,128]{2,1,0:T(8,128)(2,1)} %all-gather.6.cloned.1.call-done), kind=kOutput, calls=%fused_computation.51 | convolution fusion | flops 41996288 | bytes 1687552 | tf_op jit(solution)/shard_map/dot_general | solution.py:67
  66.5 2.4 %fusion = bf16[1,2,5120,128]{2,3,1,0:T(8,128)(2,1)} fusion(bf16[32,5120,1]{1,0,2:T(8,128)(2,1)S(1)} %reshape.190, bf16[1,32,128]{2,1,0:T(8,128)(2,1)S(1)} %get-tuple-element.21, bf16[1,32,128]{2,1,0:T(8,128)(2,1)S(1)} %get-tuple-element.20), kind=kOutput, calls=%fused_computation.3 | convolution fusion | flops 85204992 | bytes 2965504 | tf_op jit(solution)/shard_map/rd,krs->kds/dot_general | solution.py:93
  68.9 2.1 %convolution_convert_fusion.2 = bf16[32,5120]{1,0:T(8,128)(2,1)S(1)} fusion(bf16[1,5120,128]{2,1,0:T(8,128)(2,1)} %all-gather.6.cloned.1.call-done, bf16[1,32,128]{2,1,0:T(8,128)(2,1)S(1)} %multiply_convert_fusion), kind=kOutput, calls=%fused_computation.8 | convolution fusion | flops 42106880 | bytes 1646592 | tf_op jit(solution)/shard_map/rs,ds->rd/dot_general | solution.py:70
  71.0 0.9 reshape.149
  71.8 3.7 %all-to-all-start.2 = ((bf16[8,4,5120]{2,1,0:T(4,128)(2,1)}), bf16[8,4,5120]{2,1,0:T(4,128)(2,1)S(1)}, u32[]{:S(2)}, u32[]{:S(2)}) async-start(bf16[8,4,5120]{2,1,0:T(4,128)(2,1)} %reshape.149), calls=%async_computation.2 | async-start | bytes 655360 | tf_op jit(solution)/shard_map/all_to_all | solution.py:89
  75.5 0.9 fusion.2
  76.4 0.9 reshape.152
  77.3 8.1 %all-to-all-done.2 = bf16[8,4,5120]{2,1,0:T(4,128)(2,1)S(1)} async-done(((bf16[8,4,5120]{2,1,0:T(4,128)(2,1)}), bf16[8,4,5120]{2,1,0:T(4,128)(2,1)S(1)}, u32[]{:S(2)}, u32[]{:S(2)}) %all-to-all-start.2) | async-done | bytes 327712 | tf_op jit(solution)/shard_map/all_to_all | solution.py:89
  85.4 3.6 %all-to-all-start.5 = ((bf16[8,4,5120]{2,1,0:T(4,128)(2,1)}), bf16[8,4,5120]{2,1,0:T(4,128)(2,1)S(1)}, u32[]{:S(2)}, u32[]{:S(2)}) async-start(bf16[8,4,5120]{2,1,0:T(4,128)(2,1)} %reshape.152), calls=%async_computation.5 | async-start | bytes 655360 | tf_op jit(solution)/shard_map/all_to_all | solution.py:91
  89.0 0.2 fusion.14
  89.2 0.6 copy.36
  89.9 8.9 %all-to-all-done.5 = bf16[8,4,5120]{2,1,0:T(4,128)(2,1)S(1)} async-done(((bf16[8,4,5120]{2,1,0:T(4,128)(2,1)}), bf16[8,4,5120]{2,1,0:T(4,128)(2,1)S(1)}, u32[]{:S(2)}, u32[]{:S(2)}) %all-to-all-start.5) | async-done | bytes 327712 | tf_op jit(solution)/shard_map/all_to_all | solution.py:91
  98.8 0.2 fusion.12
  99.1 0.6 copy.37
  99.7 2.0 %bitcast_convert_fusion = f32[1,1280,128]{2,1,0:T(8,128)} fusion(bf16[1,1,1280,128]{3,2,1,0:T(8,128)(2,1)} %reduce-scatter.5.cloned.1.call-done), kind=kLoop, calls=%fused_computation.16 | loop fusion | flops 163840 | bytes 983040 | tf_op jit(solution)/shard_map/squeeze | solution.py:107
  101.7 25.1 %reduce-scatter.3.cloned.1.call-done = bf16[1,2,1280,128]{2,3,1,0:T(8,128)(2,1)} async-done(((bf16[1,2,5120,128]{2,3,1,0:T(8,128)(2,1)}), bf16[1,2,1280,128]{2,3,1,0:T(8,128)(2,1)}) %reduce-scatter.3.cloned.1.call-update) | async-done | bytes 655376 | tf_op jit(solution)/shard_map/reduce_scatter | solution.py:100
  126.8 2.4 %copy.17 = f32[1,2,1280,128]{3,2,1,0:T(8,128)} copy(bf16[1,2,1280,128]{2,3,1,0:T(8,128)(2,1)} %reduce-scatter.3.cloned.1.call-done) | data formatting | bytes 1966080
  (17 shorter events, 0.2 us)
Async XLA Ops:
  7.2 2.2 %copy-start = (bf16[1,4,5120]{2,1,0:T(4,128)(2,1)S(1)}, bf16[1,4,5120]{2,1,0:T(4,128)(2,1)}, u32[]{:S(2)}) copy-start(bf16[1,4,5120]{2,1,0:T(4,128)(2,1)} %param.12) | copy-start | bytes 122884
  7.2 53.6 %all-gather.4.cloned.1.call-start = ((), (), s32[]{:S(2)}) async-start(), calls=%async_computation.8 | async-start | bytes 3276800 | tf_op jit(solution)/shard_map/all_gather | solution.py:59
  13.3 8.2 %all-to-all-start = ((bf16[4,2,2560]{2,1,0:T(2,128)(2,1)}), bf16[4,2,2560]{2,1,0:T(2,128)(2,1)S(1)}, u32[]{:S(2)}, u32[]{:S(2)}) async-start(bf16[4,2,2560]{2,1,0:T(2,128)(2,1)} %reshape.197), calls=%async_computation | async-start | bytes 81920 | tf_op jit(solution)/shard_map/all_to_all | solution.py:32
  17.6 47.2 %all-gather.6.cloned.1.call-start = ((), (), s32[]{:S(2)}) async-start(), calls=%async_computation.11 | async-start | bytes 1638400 | tf_op jit(solution)/shard_map/all_gather | solution.py:60
  21.5 7.7 %all-to-all-start.3 = ((bf16[4,2,2560]{2,1,0:T(2,128)(2,1)}), bf16[4,2,2560]{2,1,0:T(2,128)(2,1)S(1)}, u32[]{:S(2)}, u32[]{:S(2)}) async-start(bf16[4,2,2560]{2,1,0:T(2,128)(2,1)} %reshape.199), calls=%async_computation.3 | async-start | bytes 81920 | tf_op jit(solution)/shard_map/all_to_all | solution.py:33
  47.5 13.1 %all-to-all-start.1 = ((bf16[8,4,5120]{2,1,0:T(4,128)(2,1)}), bf16[8,4,5120]{2,1,0:T(4,128)(2,1)S(1)}, u32[]{:S(2)}, u32[]{:S(2)}) async-start(bf16[8,4,5120]{2,1,0:T(4,128)(2,1)} %get-tuple-element.23), calls=%async_computation.1 | async-start | bytes 655360 | tf_op jit(solution)/shard_map/all_to_all | solution.py:44
  51.0 48.8 %reduce-scatter.5.cloned.1.call-start = ((), (), s32[]{:S(2)}) async-start(), calls=%async_computation.10 | async-start | bytes 1638400 | tf_op jit(solution)/shard_map/reduce_scatter | solution.py:103
  64.7 62.1 %reduce-scatter.3.cloned.1.call-start = ((), (), s32[]{:S(2)}) async-start(), calls=%async_computation.9 | async-start | bytes 3276800 | tf_op jit(solution)/shard_map/reduce_scatter | solution.py:100
  68.8 6.7 %copy-start.1 = (bf16[1,2,5120,128]{3,2,1,0:T(8,128)(2,1)S(1)}, bf16[1,2,5120,128]{3,2,1,0:T(8,128)(2,1)}, u32[]{:S(2)}) copy-start(bf16[1,2,5120,128]{3,2,1,0:T(8,128)(2,1)} %all-gather.4.cloned.1.call-done) | copy-start | bytes 7864324
  71.8 17.2 %copy-start.2 = (s32[8]{0:T(128)S(1)}, s32[8]{0:T(128)}, u32[]{:S(2)}) copy-start(s32[8]{0:T(128)} %param.15) | copy-start | bytes 100
  71.8 13.5 %all-to-all-start.2 = ((bf16[8,4,5120]{2,1,0:T(4,128)(2,1)}), bf16[8,4,5120]{2,1,0:T(4,128)(2,1)S(1)}, u32[]{:S(2)}, u32[]{:S(2)}) async-start(bf16[8,4,5120]{2,1,0:T(4,128)(2,1)} %reshape.149), calls=%async_computation.2 | async-start | bytes 655360 | tf_op jit(solution)/shard_map/all_to_all | solution.py:89
  85.4 13.5 %all-to-all-start.5 = ((bf16[8,4,5120]{2,1,0:T(4,128)(2,1)}), bf16[8,4,5120]{2,1,0:T(4,128)(2,1)S(1)}, u32[]{:S(2)}, u32[]{:S(2)}) async-start(bf16[8,4,5120]{2,1,0:T(4,128)(2,1)} %reshape.152), calls=%async_computation.5 | async-start | bytes 655360 | tf_op jit(solution)/shard_map/all_to_all | solution.py:91
Sparse Core Ops, SparseCore 0:
  9.6 28.6 all-gather.3
  39.9 18.2 all-gather.5
  64.9 24.6 reduce-scatter.4
  92.1 34.6 reduce-scatter.2
where the time goes:
time: 137 us; the launch traced here: 136 us
  waiting for transfers between devices  58.1 us (42%)
  starting transfers between devices  18.4 us (13%)
  blocking collectives  17.1 us (12%)
  between operations  14.6 us (11%)
  matrix products  11.4 us (8%)
  local copies, waits for them, and re-layouts  9.46 us (7%)
  other arithmetic  6.7 us (5%)
    reduce_scatter x1, waiting for transfers between devices, body(): lax.psum_scatter(gate_up_term[None].astype(jnp.bfloat16), 'grp', scatter_...  25.1 us
    all_to_all x1, blocking collectives, body(): lax.all_to_all(jnp.take(kept_cotangent, expert_of, axis=0), 'ep', split_a...  17.1 us
    all_to_all x1, waiting for transfers between devices, body(): lax.all_to_all(jnp.take(kept_tokens, expert_of, axis=0), 'ep', split_axis...  9.55 us
    all_to_all x1, waiting for transfers between devices, body(): lax.all_to_all(backward_part, 'ep', split_axis=0, concat_axis=0, tiled=True)  8.94 us
    all_to_all x1, waiting for transfers between devices, body(): lax.all_to_all(forward_part, 'ep', split_axis=0, concat_axis=0, tiled=True)  8.1 us
    all_to_all x1, waiting for transfers between devices, body(): lax.all_to_all(send_cotangent, 'grp', split_axis=0, concat_axis=0, tiled=...  4.34 us
    all_to_all x1, starting transfers between devices, body(): lax.all_to_all(send_tokens, 'grp', split_axis=0, concat_axis=0, tiled=True)  4.21 us
    unnamed x11, local copies, waits for them, and re-layouts  3.74 us
  transfers between devices with their start and end apart: 9, of which 6 were waited for; matrix products, arithmetic and copies ran while one was open for 19% of the time, Pallas kernels for 0%

commit v1 on v0

v1 whole, which is shorter than its diff:
```python
import functools

import jax
import jax.numpy as jnp
import numpy as np
from jax import lax
from jax.experimental import pallas as pl
from jax.experimental.pallas import tpu as pltpu
from jax.sharding import PartitionSpec as P

MESH = pl.DeviceIdType.MESH
BF16 = jnp.bfloat16
F32 = jnp.float32
PAIR = 2


def dot(a, b, contract):
    return lax.dot_general(a, b, ((contract[:1], contract[1:]), ((), ())), preferred_element_type=F32)


def kernel(
    dims,
    packed_ref, meta_ref, expert_ref, gate_up_ref, down_ref,
    rows_out, gate_up_out, down_out,
    inbox, metas, xall, weights, part, partin, grads, outrows, yin, zin, own, outbox, inbox2, gate_up_acc, down_acc,
    pack_sems, meta_sems, z_sems, y_sems, part_sems, grad_sems, yo_sems, zo_sems, out_sems, w_sems, o_sems,
):
    groups, zs, fold, tok, experts, split, per_dot = dims
    me, ep = lax.axis_index("grp"), lax.axis_index("ep")
    z, y = ep // PAIR, ep % PAIR
    other = z * PAIR + (PAIR - 1 - y)
    width, cols, slc = xall.shape[-1], inbox.shape[-1], down_acc.shape[-1]
    rows = xall.shape[3]
    blocks = PAIR * zs
    per_chunk = blocks // groups
    n_in, n_rows = groups * inbox.shape[1], 2 * rows

    loads = [
        pltpu.make_async_copy(gate_up_ref.at[0], weights.at[:, pl.ds(0, slc)], w_sems.at[0]),
        pltpu.make_async_copy(gate_up_ref.at[1], weights.at[:, pl.ds(slc, slc)], w_sems.at[1]),
        pltpu.make_async_copy(down_ref, weights.at[:, pl.ds(2 * slc, slc)], w_sems.at[2]),
    ]
    for load in loads:
        load.start()

    grp_peers = [(d, lax.rem(me + d, groups)) for d in range(1, groups)]
    z_peers = [(d, lax.rem(z + d, zs)) for d in range(1, zs)]

    barrier = pltpu.get_barrier_semaphore()
    for _, p in grp_peers:
        pl.semaphore_signal(barrier, inc=1, device_id=(p, ep), device_id_type=MESH)
    for _, q in z_peers:
        pl.semaphore_signal(barrier, inc=1, device_id=(me, q * PAIR + y), device_id_type=MESH)
    pl.semaphore_signal(barrier, inc=1, device_id=(me, other), device_id_type=MESH)
    pl.semaphore_wait(barrier, groups - 1 + zs - 1 + 1)

    def remote(src, dst, sems, at, device):
        return pltpu.make_async_remote_copy(
            src_ref=src, dst_ref=dst, send_sem=sems.at[0, at], recv_sem=sems.at[1, at],
            device_id=device, device_id_type=MESH,
        )

    sent = []

    meta_copies = [remote(meta_ref, metas.at[me], meta_sems, d, (p, ep)) for d, p in grp_peers]
    pack_copies = [remote(packed_ref.at[p], inbox.at[me], pack_sems, d, (p, ep)) for d, p in grp_peers]
    for copy in meta_copies + pack_copies:
        copy.start()
    sent += meta_copies + pack_copies
    metas[me] = meta_ref[...]
    inbox[me] = packed_ref[me]
    for copy in meta_copies:
        copy.wait_recv()

    def meta_row(g, at, count):
        return metas[g, at:at + 1, 0:count]

    dest_in = sum(meta_row(g, 0, n_in) for g in range(groups))
    dest_rows = sum(meta_row(g, 2, n_rows) for g in range(groups))
    row_of, fold_of, slot_of = (meta_ref[i:i + 1, 0:n_in] for i in (3, 4, 5))
    base = meta_ref[6:7, 0:n_rows]
    kept = sum(
        jnp.where((dest_in == h) & (slot_of < meta_row(h, 1, n_in)), 1, 0) for h in range(groups)
    )
    row_of = jnp.where(kept > 0, row_of, -1)
    row_at = lax.broadcasted_iota(jnp.int32, (n_rows, n_in), 0)
    picks_in = [
        jnp.where((row_at == row_of) & (fold_of == f), 1.0, 0.0).astype(BF16) for f in range(fold)
    ]
    out_at = lax.broadcasted_iota(jnp.int32, (n_in, n_rows), 0)
    target = dest_rows * (fold * 2 * tok) + base
    picks_out = [
        jnp.where(out_at == target + f * 2 * tok, 1.0, 0.0).astype(BF16) for f in range(fold)
    ]

    for copy in pack_copies:
        copy.wait_recv()
    arrived = inbox[...].reshape(n_in, cols)
    for f in range(fold):
        picked = dot(picks_in[f], arrived, (1, 0)).astype(BF16)
        xall[0, z, :, :, f * cols:(f + 1) * cols] = picked.reshape(2, rows, cols)

    y_own = remote(xall.at[0, z], xall.at[1, z], y_sems, 0, (me, other))
    y_own.start()
    z_copies = [
        remote(xall.at[0, z], xall.at[0, z], z_sems, d, (me, q * PAIR + y)) for d, q in z_peers
    ]
    for copy in z_copies:
        copy.start()
    y_copies = [y_own]
    for d, copy in zip(range(1, zs), z_copies):
        copy.wait_recv()
        source = lax.rem(z + zs - d, zs)
        forward = remote(xall.at[0, source], xall.at[1, source], y_sems, d, (me, other))
        forward.start()
        y_copies.append(forward)
    sent += z_copies + y_copies

    for load in loads:
        load.wait()

    def x_rows(side, first, kind):
        return xall[side, pl.ds(first, per_dot), kind].reshape(per_dot * rows, width)

    def project(side):
        def step(i, carry):
            first = i * per_dot
            gate_up = dot(x_rows(side, first, 0), weights[:, 0:2 * slc], (1, 0))
            hidden_grad = dot(x_rows(side, first, 1), weights[:, 2 * slc:3 * slc], (1, 0))
            at = pl.ds(side * zs + first, per_dot)
            part[at, :, 0:2 * slc] = gate_up.astype(BF16).reshape(per_dot, rows, 2 * slc)
            part[at, :, 2 * slc:3 * slc] = hidden_grad.astype(BF16).reshape(per_dot, rows, slc)
            return carry

        lax.fori_loop(0, zs // per_dot, step, 0)

    project(0)
    for copy in y_copies:
        copy.wait_recv()
    project(1)

    part_copies = [
        remote(part.at[pl.ds(p * per_chunk, per_chunk)], partin.at[me], part_sems, d, (p, ep))
        for d, p in grp_peers
    ]
    for copy in part_copies:
        copy.start()
    sent += part_copies
    total = part[pl.ds(me * per_chunk, per_chunk)].astype(F32)
    for d, copy in zip(range(1, groups), part_copies):
        copy.wait_recv()
        total = total + partin[lax.rem(me + groups - d, groups)].astype(F32)
    gate, up, hidden_grad = (total[:, :, i * slc:(i + 1) * slc] for i in range(3))
    sig = jax.nn.sigmoid(gate)
    activated = gate * sig
    hidden = activated * up
    gate_grad = hidden_grad * up * sig * (1.0 + gate * (1.0 - sig))
    up_grad = hidden_grad * activated
    if experts > 1:
        row = lax.broadcasted_iota(jnp.int32, gate.shape, 1)
        block = tok // groups
        slot = (row // tok) * block + row % block
        mine = slot // (tok // experts) == expert_ref[0]
        gate_grad, up_grad, hidden = (jnp.where(mine, v, 0.0) for v in (gate_grad, up_grad, hidden))
    share = pl.ds(me * per_chunk, per_chunk)
    grads[share, :, 0:slc] = gate_grad.astype(BF16)
    grads[share, :, slc:2 * slc] = up_grad.astype(BF16)
    grads[share, :, 2 * slc:3 * slc] = hidden.astype(BF16)
    grad_copies = [
        remote(grads.at[share], grads.at[share], grad_sems, d, (p, ep)) for d, p in grp_peers
    ]
    for copy in grad_copies:
        copy.start()
    sent += grad_copies
    for copy in grad_copies:
        copy.wait_recv()

    def grad_rows(side, first, low, high):
        count = (high - low) * slc
        return grads[pl.ds(side * zs + first, per_dot), :, low * slc:high * slc].reshape(per_dot * rows, count)

    def to_other(i, carry):
        first = i * per_dot
        at = pl.ds(first, per_dot)
        ahead = dot(grad_rows(1, first, 2, 3), weights[:, 2 * slc:3 * slc], (1, 1))
        back = dot(grad_rows(1, first, 0, 2), weights[:, 0:2 * slc], (1, 1))
        outrows[at, 0] = ahead.astype(BF16).reshape(per_dot, rows, width)
        outrows[at, 1] = back.astype(BF16).reshape(per_dot, rows, width)
        return carry

    lax.fori_loop(0, zs // per_dot, to_other, 0)
    order = [lax.rem(z + d, zs) for d in list(range(1, zs)) + [0]]
    yo_copies = [
        remote(outrows.at[q], yin.at[q], yo_sems, i, (me, other)) for i, q in enumerate(order)
    ]
    for copy in yo_copies:
        copy.start()

    gate_up_acc[...] = jnp.zeros_like(gate_up_acc)
    down_acc[...] = jnp.zeros_like(down_acc)
    for side in range(PAIR):
        def weight_step(i, carry, side=side):
            first = i * per_dot
            both = dot(x_rows(side, first, 0), grad_rows(side, first, 0, 2), (0, 0))
            gate_up_acc[0] += both[:, 0:slc]
            gate_up_acc[1] += both[:, slc:2 * slc]
            down_acc[...] += dot(x_rows(side, first, 1), grad_rows(side, first, 2, 3), (0, 0))
            return carry

        lax.fori_loop(0, zs // per_dot, weight_step, 0)
    stores = [
        pltpu.make_async_copy(gate_up_acc, gate_up_out, o_sems.at[0]),
        pltpu.make_async_copy(down_acc, down_out, o_sems.at[1]),
    ]
    for store in stores:
        store.start()

    zo_copies = []
    for i, q in enumerate(order):
        at = pl.ds(q, 1)
        h = grads[at, :, 2 * slc:3 * slc].reshape(rows, slc)
        gu = grads[at, :, 0:2 * slc].reshape(rows, 2 * slc)
        ahead = dot(h, weights[:, 2 * slc:3 * slc], (1, 1))
        back = dot(gu, weights[:, 0:2 * slc], (1, 1))
        yo_copies[i].wait()
        ahead = ahead + yin[q, 0].astype(F32)
        back = back + yin[q, 1].astype(F32)
        if i < zs - 1:
            outrows[q, 0] = ahead.astype(BF16)
            outrows[q, 1] = back.astype(BF16)
            copy = remote(outrows.at[q], zin.at[z], zo_sems, i + 1, (me, q * PAIR + y))
            copy.start()
            zo_copies.append(copy)
        else:
            own[0] = ahead
            own[1] = back
    sent += zo_copies
    for d, copy in zip(range(1, zs), zo_copies):
        copy.wait_recv()
        own[...] += zin[lax.rem(z + zs - d, zs)].astype(F32)

    final = own[...].astype(BF16).reshape(n_rows, width)
    placed = sum(
        dot(picks_out[f], final[:, f * cols:(f + 1) * cols], (1, 0)) for f in range(fold)
    )
    outbox[...] = placed.astype(BF16).reshape(outbox.shape)
    out_copies = [remote(outbox.at[p], inbox2.at[me], out_sems, d, (p, ep)) for d, p in grp_peers]
    for copy in out_copies:
        copy.start()
    sent += out_copies
    inbox2[me] = outbox[me]
    for copy in out_copies:
        copy.wait_recv()
    rows_out[...] = inbox2[...]
    for store in stores:
        store.wait()
    for copy in sent:
        copy.wait_send()


def body(tokens, cotangent, counts, destination, placement, gate_up_weight, down_weight):
    groups = lax.axis_size("grp")
    owners = lax.axis_size("ep")
    me, ep = lax.axis_index("grp"), lax.axis_index("ep")
    tok, model = tokens.shape[1], tokens.shape[2]
    experts = counts.shape[2]
    cap = tok // experts
    block = tok // groups
    split = owners // experts
    width, slc = down_weight.shape[1], down_weight.shape[2]
    zs = owners // PAIR
    fold = max(1, 16 // (2 * tok))
    cols = width // fold
    box = fold * 2 * tok
    rows = groups * tok
    n_in, n_rows = groups * box, 2 * rows
    per_dot = min(zs, max(1, 64 // rows))
    lanes = -(-max(n_in, n_rows) // 128) * 128

    def pad(values, fill):
        return np.concatenate([values, np.full(lanes - len(values), fill)]).astype(np.int32)

    g_i, f_i, t_i, q_i = (v.ravel() for v in np.indices((groups, fold, 2, tok)))
    t_m, g_m, q_m = (v.ravel() for v in np.indices((2, groups, tok)))
    slot_i = g_i * block + q_i % block
    slot_m = g_m * block + q_m % block
    dest = destination[0, 0]
    kept_count = counts[0, 0]
    zero = np.zeros(lanes, np.int32)
    meta = jnp.stack([
        jnp.where(pad(g_i, -1) == me, dest[pad(q_i // block, 0)], 0),
        kept_count[pad(slot_i // cap, 0)],
        jnp.where(pad(g_m, -1) == me, dest[pad(q_m // block, 0)], 0),
        pad(t_i * rows + g_i * tok + q_i, -1),
        pad(f_i, -1),
        pad(slot_i % cap, 0),
        pad(t_m * tok + slot_m, 0),
        zero,
    ])
    packed = jnp.stack([tokens[0], cotangent[0]]).reshape(2, tok, groups, fold, cols)
    packed = jnp.transpose(packed, (2, 3, 0, 1, 4)).reshape(groups, box, cols)
    expert = lax.dynamic_slice(placement // split, (ep,), (1,))

    blocks = PAIR * zs
    per_chunk = blocks // groups
    vmem = pl.BlockSpec(memory_space=pltpu.VMEM)
    anywhere = pl.BlockSpec(memory_space=pl.ANY)
    shapes = [
        ((groups, box, cols), BF16),
        ((groups, 8, lanes), jnp.int32),
        ((PAIR, zs, 2, rows, width), BF16),
        ((width, 3 * slc), BF16),
        ((blocks, rows, 3 * slc), BF16),
        ((groups, per_chunk, rows, 3 * slc), BF16),
        ((blocks, rows, 3 * slc), BF16),
        ((zs, 2, rows, width), BF16),
        ((zs, 2, rows, width), BF16),
        ((zs, 2, rows, width), BF16),
        ((2, rows, width), F32),
        ((groups, box, cols), BF16),
        ((groups, box, cols), BF16),
        ((2, width, slc), F32),
        ((width, slc), F32),
    ]
    held = sum(
        int(np.prod(s[:-1])) * (-(-s[-1] // 128) * 128) * np.dtype(t).itemsize for s, t in shapes
    )
    dma = pltpu.SemaphoreType.DMA
    out, gate_up_grad, down_grad = pl.pallas_call(
        functools.partial(kernel, (groups, zs, fold, tok, experts, split, per_dot)),
        out_shape=(
            jax.ShapeDtypeStruct((groups, box, cols), BF16),
            jax.ShapeDtypeStruct((2, width, slc), F32),
            jax.ShapeDtypeStruct((width, slc), F32),
        ),
        in_specs=[vmem, vmem, pl.BlockSpec(memory_space=pltpu.SMEM), anywhere, anywhere],
        out_specs=(vmem, anywhere, anywhere),
        scratch_shapes=[pltpu.VMEM(s, t) for s, t in shapes] + [
            dma((2, groups)), dma((2, groups)), dma((2, zs)), dma((2, zs)), dma((2, groups)),
            dma((2, groups)), dma((2, zs)), dma((2, zs)), dma((2, groups)), dma((3,)), dma((2,)),
        ],
        compiler_params=pltpu.CompilerParams(
            collective_id=0, has_side_effects=True, vmem_limit_bytes=min(held + (12 << 20), 62 << 20)
        ),
    )(packed, meta, expert, gate_up_weight[0], down_weight[0])
    out = out.reshape(groups, fold, 2, tok, cols)
    out = jnp.transpose(out, (2, 3, 0, 1, 4)).reshape(2, 1, tok, model)
    return out[0], out[1], gate_up_grad[None], down_grad[None]


def solution(mesh):
    return jax.shard_map(
        body,
        mesh=mesh,
        in_specs=(
            P("grp", "ep", None),
            P("grp", "ep", None),
            P("grp", "ep", None),
            P("grp", "ep", None),
            P(),
            P("ep", None, "grp", None),
            P("ep", "grp", None),
        ),
        out_specs=(
            P("grp", "ep", None),
            P("grp", "ep", None),
            P("ep", None, "grp", None),
            P("ep", "grp", None),
        ),
        check_vma=False,
    )
```

time: 137 us -> 58.4 us (0.43)
  waiting for transfers between devices: 58.1 us -> 0 us
  Pallas kernels: 0 us -> 44.4 us
  starting transfers between devices: 18.4 us -> 0 us
  blocking collectives: 17.1 us -> 0 us
  between operations: 14.6 us -> 1.34 us
  matrix products: 11.4 us -> 0 us
  local copies, waits for them, and re-layouts: 9.46 us -> 7.43 us
  other arithmetic: 6.7 us -> 4.88 us
    pallas_call x0 -> x1, Pallas kernels: none -> 44.4 us  [body(): pl.pallas_call(functools.partial(kernel, (groups, zs, fold, tok, experts,...]
    all_to_all x5 -> x0, waiting for transfers between devices: 31.5 us -> none  [the longest x1 9.55 us: body(): lax.all_to_all(jnp.take(kept_tokens, expert_of, axis=0), 'ep', split_axis...]
    reduce_scatter x2 -> x0, waiting for transfers between devices: 25.1 us -> none  [the longest x1 25.1 us: body(): lax.psum_scatter(gate_up_term[None].astype(jnp.bfloat16), 'grp', scatter_...]
    all_to_all x5 -> x0, starting transfers between devices: 18.2 us -> none  [the longest x1 4.21 us: body(): lax.all_to_all(send_tokens, 'grp', split_axis=0, concat_axis=0, tiled=True)]
    all_to_all x1 -> x0, blocking collectives: 17.1 us -> none  [body(): lax.all_to_all(jnp.take(kept_cotangent, expert_of, axis=0), 'ep', split_a...]
    dot_general x8 -> x0, matrix products: 11.4 us -> none  [the longest x1 2.38 us: body(): jnp.einsum('rd,krs->kds', routed_tokens, grad_rows, preferred_element_typ...]
    another operation x0 -> x2, other arithmetic: none -> 4.22 us  [the longest x1 3.36 us: body(): jnp.stack([jnp.where(pad(g_i, -1) == me, dest[pad(q_i // block, 0)], 0),...]
    squeeze x1 -> x0, other arithmetic: 1.96 us -> none  [body(): return (layer_out, input_grad, gate_up_grad, down_grad[:, 0])]
  transfers between devices with their start and end apart: 9 -> 0, of which waited for: 6 -> 0; matrix products, arithmetic and copies ran while one was open for 19% -> 0% of each run, Pallas kernels for 0% -> 0%
where the time goes in v1:
time: 58.4 us; the launch traced here: 58.1 us
  Pallas kernels  44.4 us (76%)
  local copies, waits for them, and re-layouts  7.43 us (13%)
  other arithmetic  4.88 us (8%)
  between operations  1.34 us (2%)
    pallas_call x1, Pallas kernels, body(): pl.pallas_call(functools.partial(kernel, (groups, zs, fold, tok, experts,...  44.4 us
    unnamed x6, local copies, waits for them, and re-layouts  3.95 us
    another operation x1, other arithmetic, body(): jnp.stack([jnp.where(pad(g_i, -1) == me, dest[pad(q_i // block, 0)], 0),...  3.36 us
    gather x1, local copies, waits for them, and re-layouts, body(): dest[pad(q_i // block, 0)]  1.39 us

profile of v1, /device:TPU:0, one launch (start us, length us, event | category | flops | bytes accessed | tf_op | source)
XLA Modules:
  0.0 58.1 jit_solution(5723715854793359820)
XLA Ops:
  1.3 0.7 %and_select_fusion = s32[8]{0:T(128)S(1)} fusion(s32[8]{0:T(128)} %param.22), kind=kLoop, calls=%fused_computation.2 | loop fusion | flops 120 | bytes 64 | tf_op jit(solution)/shard_map/jit(floor_divide)/jit(_where)/select_n | solution.py:302
  2.0 0.6 dynamic_slice.3.expert_ref
  2.5 1.4 %fusion.3 = (s32[1,1,1]{2,1,0:T(1,128)}, s32[1,1,1]{2,1,0:T(1,128)}, s32[1,1,1]{2,1,0:T(1,128)}, s32[1,1,1]{2,1,0:T(1,128)}) fusion(s32[1,1,4]{2,1,0:T(1,128)} %param.21), kind=kLoop, calls=%fused_computation.11 | loop fusion | bytes 32 | tf_op jit(solution)/shard_map/gather | solution.py:291
  3.9 3.4 %fusion = (s32[1,128]{1,0:T(1,128)S(1)}, s32[1,128]{1,0:T(1,128)S(1)}) fusion(s32[128]{0:T(128)} %constant.49.clone, pred[128]{0:T(512)(128)(4,1)} %constant.80, pred[128]{0:T(512)(128)(4,1)} %constant.81, pred[128]{0:T(512)(128)(4,1)} %constant.82, s32[]{:T(128)} %bitcast.4, s32[]{:T(128)} %bitcast.1, s32[]{:T(128)} %bitcast.2, s32[]{:T(128)} %bitcast.3, ...), kind=kLoop, calls=%fused_computation.8 | loop fusion | flops 1280 | bytes 2836 | tf_op jit(solution)/shard_map/stack | solution.py:290
  7.3 0.7 %stack.39.meta_ref = s32[8,128]{1,0:T(8,128)S(1)} concatenate(s32[1,128]{1,0:T(1,128)S(1)} %get-tuple-element.16, s32[1,128]{1,0:T(1,128)S(1)} %stack.32, s32[1,128]{1,0:T(1,128)S(1)} %get-tuple-element.17, s32[1,128]{1,0:T(1,128)} %constant.67, s32[1,128]{1,0:T(1,128)} %constant.68, s32[1,128]{1,0:T(1,128)} %constant.69, s32[1,128]{1,0:T(1,128)} %constant.70, ...), dimensions={0} | concatenate | bytes 8192 | tf_op jit(solution)/shard_map/stack | solution.py:290
  8.0 0.9 %pad_maximum_fusion = bf16[2,4,5120]{2,1,0:T(4,128)(2,1)S(1)} fusion(bf16[1,4,5120]{2,1,0:T(4,128)(2,1)} %param.19, bf16[1,4,5120]{2,1,0:T(4,128)(2,1)} %param.18), kind=kLoop, calls=%fused_computation | loop fusion | flops 40960 | bytes 163840 | tf_op jit(solution)/shard_map/stack | solution.py:300
  9.0 0.0 copy-start
  9.0 1.1 %copy-done = bf16[1,2,1280,128]{3,2,1,0:T(8,128)(2,1)S(1)} copy-done((bf16[1,2,1280,128]{3,2,1,0:T(8,128)(2,1)S(1)}, bf16[1,2,1280,128]{3,2,1,0:T(8,128)(2,1)}, u32[]{:S(2)}) %copy-start) | copy-done | bytes 655384
  10.1 0.0 copy-start.1
  10.1 1.0 %copy-done.1 = bf16[1,1280,128]{2,1,0:T(8,128)(2,1)S(1)} copy-done((bf16[1,1280,128]{2,1,0:T(8,128)(2,1)S(1)}, bf16[1,1280,128]{2,1,0:T(8,128)(2,1)}, u32[]{:S(2)}) %copy-start.1) | copy-done | bytes 327704
  11.1 44.4 %shard_map.211 = (bf16[4,16,640]{2,1,0:T(8,128)(2,1)S(1)}, f32[2,1280,128]{2,1,0:T(8,128)S(1)}, f32[1280,128]{1,0:T(8,128)S(1)}) custom-call(bf16[4,16,640]{2,1,0:T(8,128)(2,1)S(1)} %reshape.25.packed_ref, s32[8,128]{1,0:T(8,128)S(1)} %stack.39.meta_ref, s32[1]{0:T(128)} %dynamic_slice.3.expert_ref, bf16[2,1280,128]{2,1,0:T(8,128)(2,1)S(1)} %bitcast.22, ...), custom_call_target="tpu_custom_call" | custom-call | tf_op jit(solution)/shard_map/pallas_call | solution.py:329
  55.5 0.7 %fusion.2 = (bf16[1,4,4,2,640]{4,1,0,3,2:T(4,128)(2,1)}, bf16[1,4,4,2,640]{4,1,0,3,2:T(4,128)(2,1)}) fusion(bf16[2,4,4,2,640]{4,1,0,3,2:T(4,128)(2,1)S(1)} %bitcast.24), kind=kLoop, calls=%fused_computation.10 | loop fusion | bytes 163840 | tf_op jit(solution)/shard_map/slice | solution.py:348
  56.2 1.1 %copy.30 = f32[1,2,1280,128]{3,2,1,0:T(8,128)} copy(f32[1,2,1280,128]{3,2,1,0:T(8,128)S(1)} %bitcast.20) | data formatting | bytes 2621440
  57.2 0.8 %copy.31 = f32[1,1280,128]{2,1,0:T(8,128)} copy(f32[1,1280,128]{2,1,0:T(8,128)S(1)} %bitcast.21) | data formatting | bytes 1310720
  (6 shorter events, 0.1 us)
Async XLA Ops:
  9.0 1.1 %copy-start = (bf16[1,2,1280,128]{3,2,1,0:T(8,128)(2,1)S(1)}, bf16[1,2,1280,128]{3,2,1,0:T(8,128)(2,1)}, u32[]{:S(2)}) copy-start(bf16[1,2,1280,128]{3,2,1,0:T(8,128)(2,1)} %param.23) | copy-start | bytes 1966084
  10.1 1.0 %copy-start.1 = (bf16[1,1280,128]{2,1,0:T(8,128)(2,1)S(1)}, bf16[1,1280,128]{2,1,0:T(8,128)(2,1)}, u32[]{:S(2)}) copy-start(bf16[1,1280,128]{2,1,0:T(8,128)(2,1)} %param.24) | copy-start | bytes 983044

commit v2 on v1

v2 whole, which is shorter than its diff:
```python
import functools

import jax
import jax.numpy as jnp
import numpy as np
from jax import lax
from jax.experimental import pallas as pl
from jax.experimental.pallas import tpu as pltpu
from jax.sharding import PartitionSpec as P

MESH = pl.DeviceIdType.MESH
BF16 = jnp.bfloat16
F32 = jnp.float32
PAIR = 2


def dot(a, b, contract):
    return lax.dot_general(a, b, ((contract[:1], contract[1:]), ((), ())), preferred_element_type=F32)


def kernel(
    dims,
    packed_ref, dest_ref, counts_ref, placement_ref, gate_up_ref, down_ref,
    rows_out, gate_up_out, down_out,
    inbox, metas, xall, weights, part, partin, grads, outrows, mine, yin, zin, own, outbox, inbox2, gate_up_acc, down_acc,
    pack_sems, meta_sems, z_sems, y_sems, part_sems, grad_sems, yo_sems, zo_sems, out_sems, w_sems, o_sems,
):
    groups, zs, fold, tok, experts, split, per_dot = dims
    me, ep = lax.axis_index("grp"), lax.axis_index("ep")
    z, y = ep // PAIR, ep % PAIR
    other = z * PAIR + (PAIR - 1 - y)
    width, cols, slc = xall.shape[-1], inbox.shape[-1], down_acc.shape[-1]
    rows = xall.shape[3]
    block, cap = tok // groups, tok // experts
    share = zs // groups
    box = inbox.shape[1]
    n_in, n_rows = groups * box, 2 * rows

    grp_peers = [(d, lax.rem(me + d, groups)) for d in range(1, groups)]
    z_peers = [(d, lax.rem(z + d, zs)) for d in range(1, zs)]

    barrier = pltpu.get_barrier_semaphore()
    for _, p in grp_peers:
        pl.semaphore_signal(barrier, inc=1, device_id=(p, ep), device_id_type=MESH)
    for _, q in z_peers:
        pl.semaphore_signal(barrier, inc=1, device_id=(me, q * PAIR + y), device_id_type=MESH)
    pl.semaphore_signal(barrier, inc=1, device_id=(me, other), device_id_type=MESH)

    loads = [
        pltpu.make_async_copy(gate_up_ref.at[0], weights.at[:, pl.ds(0, slc)], w_sems.at[0]),
        pltpu.make_async_copy(gate_up_ref.at[1], weights.at[:, pl.ds(slc, slc)], w_sems.at[1]),
        pltpu.make_async_copy(down_ref, weights.at[:, pl.ds(2 * slc, slc)], w_sems.at[2]),
    ]
    for load in loads:
        load.start()

    lanes = metas.shape[-1]
    lane = lax.broadcasted_iota(jnp.int32, (8, lanes), 1)
    line = lax.broadcasted_iota(jnp.int32, (8, lanes), 0)

    def slots(group, row):
        return group * block + lax.rem(row, block)

    lane_block = lax.div(lax.rem(lane, tok), block)
    lane_expert = lax.div(slots(lax.div(lane, box), lax.rem(lane, tok)), cap)
    own_dest = sum(jnp.where(lane_block == b, dest_ref[0, 0, b], 0) for b in range(groups))
    own_count = sum(jnp.where(lane_expert == e, counts_ref[0, 0, e], 0) for e in range(experts))
    metas[me] = jnp.where(line == 0, own_dest, own_count)
    inbox[me] = packed_ref[me]

    pl.semaphore_wait(barrier, groups - 1 + zs - 1 + 1)

    def remote(src, dst, sems, at, device):
        return pltpu.make_async_remote_copy(
            src_ref=src, dst_ref=dst, send_sem=sems.at[0, at], recv_sem=sems.at[1, at],
            device_id=device, device_id_type=MESH,
        )

    sent = []

    meta_copies = [remote(metas.at[me], metas.at[me], meta_sems, d, (p, ep)) for d, p in grp_peers]
    pack_copies = [remote(packed_ref.at[p], inbox.at[me], pack_sems, d, (p, ep)) for d, p in grp_peers]
    for copy in meta_copies + pack_copies:
        copy.start()
    sent += meta_copies + pack_copies

    n = lax.broadcasted_iota(jnp.int32, (1, n_in), 1)
    n_group, n_row = lax.div(n, box), lax.rem(n, tok)
    n_fold = lax.div(lax.rem(n, box), 2 * tok)
    row_of = lax.rem(lax.div(n, tok), 2) * rows + n_group * tok + n_row
    slot_of = lax.rem(slots(n_group, n_row), cap)
    m = lax.broadcasted_iota(jnp.int32, (1, n_rows), 1)
    m_group = lax.rem(lax.div(m, tok), groups)
    base = lax.div(m, rows) * tok + slots(m_group, lax.rem(m, tok))
    row_at = lax.broadcasted_iota(jnp.int32, (n_rows, n_in), 0)
    out_at = lax.broadcasted_iota(jnp.int32, (n_in, n_rows), 0)

    for copy in meta_copies:
        copy.wait_recv()
    dest_in = sum(jnp.where(n_group == g, metas[g, 0:1, 0:n_in], 0) for g in range(groups))
    dest_rows = sum(jnp.where(m_group == g, metas[g, 0:1, 0:n_rows], 0) for g in range(groups))
    kept = sum(
        jnp.where((dest_in == h) & (slot_of < metas[h, 1:2, 0:n_in]), 1, 0) for h in range(groups)
    )
    row_of = jnp.where(kept > 0, row_of, -1)
    picks_in = [
        jnp.where((row_at == row_of) & (n_fold == f), 1.0, 0.0).astype(BF16) for f in range(fold)
    ]

    for copy in pack_copies:
        copy.wait_recv()
    arrived = inbox[...].reshape(n_in, cols)
    for f in range(fold):
        picked = dot(picks_in[f], arrived, (1, 0)).astype(BF16)
        xall[0, z, :, :, f * cols:(f + 1) * cols] = picked.reshape(2, rows, cols)

    z_copies, y_copies = [[], []], [[], []]
    for t in range(2):
        y_copies[t].append(remote(xall.at[0, z, t], xall.at[1, z, t], y_sems, t * zs, (me, other)))
        z_copies[t] = [
            remote(xall.at[0, z, t], xall.at[0, z, t], z_sems, t * zs + d, (me, q * PAIR + y))
            for d, q in z_peers
        ]
        for copy in y_copies[t] + z_copies[t]:
            copy.start()

    def pass_on(t):
        for d, copy in zip(range(1, zs), z_copies[t]):
            copy.wait_recv()
            source = lax.rem(z + zs - d, zs)
            forward = remote(
                xall.at[0, source, t], xall.at[1, source, t], y_sems, t * zs + d, (me, other)
            )
            forward.start()
            y_copies[t].append(forward)

    def x_rows(side, first, kind):
        return xall[side, pl.ds(first, per_dot), kind].reshape(per_dot * rows, width)

    def project(side, kind):
        low, high = ((0, 2), (2, 3))[kind]

        def step(i, carry):
            first = i * per_dot
            out = dot(x_rows(side, first, kind), weights[:, low * slc:high * slc], (1, 0))
            part[side, pl.ds(first, per_dot), :, low * slc:high * slc] = (
                out.astype(BF16).reshape(per_dot, rows, (high - low) * slc)
            )
            return carry

        lax.fori_loop(0, zs // per_dot, step, 0)

    def send_parts(side):
        copies = [
            remote(
                part.at[side, pl.ds(p * share, share)], partin.at[side, me],
                part_sems, side * groups + d, (p, ep),
            )
            for d, p in grp_peers
        ]
        for copy in copies:
            copy.start()
        return copies

    held = pl.ds(me * share, share)

    def activate(side, copies):
        total = part[side, held].astype(F32)
        for d, copy in zip(range(1, groups), copies):
            copy.wait_recv()
            total = total + partin[side, lax.rem(me + groups - d, groups)].astype(F32)
        gate, up, hidden_grad = (total[:, :, i * slc:(i + 1) * slc] for i in range(3))
        sig = jax.nn.sigmoid(gate)
        activated = gate * sig
        hidden = activated * up
        gate_grad = hidden_grad * up * sig * (1.0 + gate * (1.0 - sig))
        up_grad = hidden_grad * activated
        if experts > 1:
            row = lax.broadcasted_iota(jnp.int32, gate.shape, 1)
            slot = slots(lax.div(row, tok), lax.rem(row, tok))
            served = lax.div(slot, cap) == lax.div(placement_ref[ep], split)
            gate_grad, up_grad, hidden = (
                jnp.where(served, v, 0.0) for v in (gate_grad, up_grad, hidden)
            )
        grads[side, held, :, 0:slc] = gate_grad.astype(BF16)
        grads[side, held, :, slc:2 * slc] = up_grad.astype(BF16)
        grads[side, held, :, 2 * slc:3 * slc] = hidden.astype(BF16)
        result = [
            remote(
                grads.at[side, held], grads.at[side, held],
                grad_sems, side * groups + d, (p, ep),
            )
            for d, p in grp_peers
        ]
        for copy in result:
            copy.start()
        return result

    def grad_rows(side, first, low, high):
        count = (high - low) * slc
        return grads[side, pl.ds(first, per_dot), :, low * slc:high * slc].reshape(per_dot * rows, count)

    def produce(side, target):
        def step(i, carry):
            first = i * per_dot
            at = pl.ds(first, per_dot)
            ahead = dot(grad_rows(side, first, 2, 3), weights[:, 2 * slc:3 * slc], (1, 1))
            target[at, 0] = ahead.astype(target.dtype).reshape(per_dot, rows, width)
            back = dot(grad_rows(side, first, 0, 2), weights[:, 0:2 * slc], (1, 1))
            target[at, 1] = back.astype(target.dtype).reshape(per_dot, rows, width)
            return carry

        lax.fori_loop(0, zs // per_dot, step, 0)

    def weight_grads(side):
        def step(i, carry):
            first = i * per_dot
            both = dot(x_rows(side, first, 0), grad_rows(side, first, 0, 2), (0, 0))
            down = dot(x_rows(side, first, 1), grad_rows(side, first, 2, 3), (0, 0))
            if side == 0 and zs == per_dot:
                gate_up_acc[0] = both[:, 0:slc]
                gate_up_acc[1] = both[:, slc:2 * slc]
                down_acc[...] = down
            else:
                gate_up_acc[0] += both[:, 0:slc]
                gate_up_acc[1] += both[:, slc:2 * slc]
                down_acc[...] += down
            return carry

        if side == 0 and zs != per_dot:
            gate_up_acc[...] = jnp.zeros_like(gate_up_acc)
            down_acc[...] = jnp.zeros_like(down_acc)
        lax.fori_loop(0, zs // per_dot, step, 0)

    pass_on(0)
    for load in loads:
        load.wait()
    project(0, 0)
    pass_on(1)
    project(0, 1)
    first_parts = send_parts(0)
    first_grads = activate(0, first_parts)
    for t in range(2):
        for copy in y_copies[t]:
            copy.wait_recv()
        project(1, t)
    second_parts = send_parts(1)
    for copy in first_grads:
        copy.wait_recv()
    produce(0, mine)
    second_grads = activate(1, second_parts)
    weight_grads(0)
    for copy in second_grads:
        copy.wait_recv()
    for t in range(2):
        sent += z_copies[t] + y_copies[t]
    sent += first_parts + second_parts + first_grads + second_grads

    produce(1, outrows)
    order = [lax.rem(z + d, zs) for d in list(range(1, zs)) + [0]]
    yo_copies = [
        remote(outrows.at[q], yin.at[q], yo_sems, i, (me, other)) for i, q in enumerate(order)
    ]
    for copy in yo_copies:
        copy.start()
    zo_copies = []
    for i, q in enumerate(order):
        yo_copies[i].wait()
        if i < zs - 1:
            outrows[q] = (mine[q].astype(F32) + yin[q].astype(F32)).astype(BF16)
            copy = remote(outrows.at[q], zin.at[z], zo_sems, i + 1, (me, q * PAIR + y))
            copy.start()
            zo_copies.append(copy)
        else:
            own[...] = mine[q].astype(F32) + yin[q].astype(F32)
    sent += zo_copies

    weight_grads(1)
    stores = [
        pltpu.make_async_copy(gate_up_acc, gate_up_out, o_sems.at[0]),
        pltpu.make_async_copy(down_acc, down_out, o_sems.at[1]),
    ]
    for store in stores:
        store.start()
    target = dest_rows * (fold * 2 * tok) + base
    picks_out = [
        jnp.where(out_at == target + f * 2 * tok, 1.0, 0.0).astype(BF16) for f in range(fold)
    ]

    for d, copy in zip(range(1, zs), zo_copies):
        copy.wait_recv()
        own[...] += zin[lax.rem(z + zs - d, zs)].astype(F32)

    final = own[...].astype(BF16).reshape(n_rows, width)
    placed = sum(
        dot(picks_out[f], final[:, f * cols:(f + 1) * cols], (1, 0)) for f in range(fold)
    )
    outbox[...] = placed.astype(BF16).reshape(outbox.shape)
    out_copies = [remote(outbox.at[p], inbox2.at[me], out_sems, d, (p, ep)) for d, p in grp_peers]
    for copy in out_copies:
        copy.start()
    sent += out_copies
    inbox2[me] = outbox[me]
    for copy in out_copies:
        copy.wait_recv()
    rows_out[...] = inbox2[...]
    for store in stores:
        store.wait()
    for copy in sent:
        copy.wait_send()


def body(tokens, cotangent, counts, destination, placement, gate_up_weight, down_weight):
    groups = lax.axis_size("grp")
    owners = lax.axis_size("ep")
    tok, model = tokens.shape[1], tokens.shape[2]
    experts = counts.shape[2]
    split = owners // experts
    width, slc = down_weight.shape[1], down_weight.shape[2]
    zs = owners // PAIR
    fold = max(1, 16 // (2 * tok))
    cols = width // fold
    box = fold * 2 * tok
    rows = groups * tok
    n_in, n_rows = groups * box, 2 * rows
    per_dot = min(zs, max(1, 64 // rows))
    lanes = -(-max(n_in, n_rows) // 128) * 128

    packed = jnp.stack([tokens[0], cotangent[0]]).reshape(2, tok, groups, fold, cols)
    packed = jnp.transpose(packed, (2, 3, 0, 1, 4)).reshape(groups, box, cols)

    share = zs // groups
    vmem = pl.BlockSpec(memory_space=pltpu.VMEM)
    smem = pl.BlockSpec(memory_space=pltpu.SMEM)
    anywhere = pl.BlockSpec(memory_space=pl.ANY)
    shapes = [
        ((groups, box, cols), BF16),
        ((groups, 8, lanes), jnp.int32),
        ((PAIR, zs, 2, rows, width), BF16),
        ((width, 3 * slc), BF16),
        ((PAIR, zs, rows, 3 * slc), BF16),
        ((PAIR, groups, share, rows, 3 * slc), BF16),
        ((PAIR, zs, rows, 3 * slc), BF16),
        ((zs, 2, rows, width), BF16),
        ((zs, 2, rows, width), F32 if zs * rows * width < (1 << 20) else BF16),
        ((zs, 2, rows, width), BF16),
        ((zs, 2, rows, width), BF16),
        ((2, rows, width), F32),
        ((groups, box, cols), BF16),
        ((groups, box, cols), BF16),
        ((2, width, slc), F32),
        ((width, slc), F32),
    ]
    dma = pltpu.SemaphoreType.DMA
    out, gate_up_grad, down_grad = pl.pallas_call(
        functools.partial(kernel, (groups, zs, fold, tok, experts, split, per_dot)),
        out_shape=(
            jax.ShapeDtypeStruct((groups, box, cols), BF16),
            jax.ShapeDtypeStruct((2, width, slc), F32),
            jax.ShapeDtypeStruct((width, slc), F32),
        ),
        in_specs=[vmem, smem, smem, smem, anywhere, anywhere],
        out_specs=(vmem, anywhere, anywhere),
        scratch_shapes=[pltpu.VMEM(s, t) for s, t in shapes] + [
            dma((2, groups)), dma((2, groups)), dma((2, 2 * zs)), dma((2, 2 * zs)), dma((2, PAIR * groups)),
            dma((2, PAIR * groups)), dma((2, zs)), dma((2, zs)), dma((2, groups)), dma((3,)), dma((2,)),
        ],
        compiler_params=pltpu.CompilerParams(
            collective_id=0, has_side_effects=True, vmem_limit_bytes=60 << 20
        ),
    )(packed, destination, counts, placement, gate_up_weight[0], down_weight[0])
    out = out.reshape(groups, fold, 2, tok, cols)
    out = jnp.transpose(out, (2, 3, 0, 1, 4)).reshape(2, 1, tok, model)
    return out[0], out[1], gate_up_grad[None], down_grad[None]


def solution(mesh):
    return jax.shard_map(
        body,
        mesh=mesh,
        in_specs=(
            P("grp", "ep", None),
            P("grp", "ep", None),
            P("grp", "ep", None),
            P("grp", "ep", None),
            P(),
            P("ep", None, "grp", None),
            P("ep", "grp", None),
        ),
        out_specs=(
            P("grp", "ep", None),
            P("grp", "ep", None),
            P("ep", None, "grp", None),
            P("ep", "grp", None),
        ),
        check_vma=False,
    )
```

time: 58.4 us -> 53.4 us (0.914)
  other arithmetic: 4.88 us -> 0.86 us
  local copies, waits for them, and re-layouts: 7.43 us -> 5.66 us
  Pallas kernels: 44.4 us -> 45.3 us
    another operation x1 -> x0, other arithmetic: 3.36 us -> none  [body(): jnp.stack([jnp.where(pad(g_i, -1) == me, dest[pad(q_i // block, 0)], 0),...]
    gather x1 -> x0, local copies, waits for them, and re-layouts: 1.39 us -> none  [body(): dest[pad(q_i // block, 0)]]
    pallas_call x1, Pallas kernels: 44.4 us -> 45.3 us  [body(): pl.pallas_call(functools.partial(kernel, (groups, zs, fold, tok, experts,...]
    reshape x1, local copies, waits for them, and re-layouts: 0.02 us -> 0.91 us  [body(): out = out.reshape(groups, fold, 2, tok, cols)]
    another operation x3 -> x0, local copies, waits for them, and re-layouts: 0.73 us -> none  [body(): jnp.stack([jnp.where(pad(g_i, -1) == me, dest[pad(q_i // block, 0)], 0),...]
    select_n x1 -> x0, other arithmetic: 0.67 us -> none  [body(): expert = lax.dynamic_slice(placement // split, (ep,), (1,))]
    reshape x1, local copies, waits for them, and re-layouts: 0.02 us -> 0.66 us  [body(): packed = jnp.transpose(packed, (2, 3, 0, 1, 4)).reshape(groups, box, cols)]
    unnamed x6 -> x4, local copies, waits for them, and re-layouts: 3.95 us -> 3.36 us
where the time goes in v2:
time: 53.4 us; the launch traced here: 53.1 us
  Pallas kernels  45.3 us (85%)
  local copies, waits for them, and re-layouts  5.66 us (11%)
  between operations  1.31 us (2%)
  other arithmetic  0.86 us (2%)
    pallas_call x1, Pallas kernels, body(): pl.pallas_call(functools.partial(kernel, (groups, zs, fold, tok, experts,...  45.3 us
    unnamed x4, local copies, waits for them, and re-layouts  3.36 us

profile of v2, /device:TPU:0, one launch (start us, length us, event | category | flops | bytes accessed | tf_op | source)
XLA Modules:
  0.0 53.1 jit_solution(7738089409191622758)
XLA Ops:
  1.3 0.9 %pad_maximum_fusion = bf16[2,4,5120]{2,1,0:T(4,128)(2,1)S(1)} fusion(bf16[1,4,5120]{2,1,0:T(4,128)(2,1)} %param.8, bf16[1,4,5120]{2,1,0:T(4,128)(2,1)} %param.7), kind=kLoop, calls=%fused_computation | loop fusion | flops 40960 | bytes 163840 | tf_op jit(solution)/shard_map/stack | solution.py:329
  2.2 0.7 %reshape.23.packed_ref = bf16[4,16,640]{2,1,0:T(8,128)(2,1)} reshape(bf16[4,2,2,4,640]{4,3,2,1,0:T(4,128)(2,1)S(1)} %bitcast.15) | data formatting | bytes 163840 | tf_op jit(solution)/shard_map/reshape | solution.py:330
  2.9 45.3 %shard_map.102 = (bf16[4,16,640]{2,1,0:T(8,128)(2,1)}, f32[2,1280,128]{2,1,0:T(8,128)}, f32[1280,128]{1,0:T(8,128)}) custom-call(bf16[4,16,640]{2,1,0:T(8,128)(2,1)} %reshape.23.packed_ref, s32[1,1,4]{2,1,0:T(1,128)} %dest_ref.1, s32[1,1,1]{2,1,0:T(1,128)S(6)} %copy.18.counts_ref, s32[8]{0:T(128)} %placement_ref.1, bf16[2,1280,128]{2,1,0:T(8,128)(2,1)} %bitcast.11, ...), custom_call_target="tpu_custom_call" | custom-call | tf_op jit(solution)/shard_map/pallas_call | solution.py:355
  48.2 0.9 %reshape.24 = bf16[4,2,2,4,640]{4,3,2,1,0:T(4,128)(2,1)S(1)} reshape(bf16[4,16,640]{2,1,0:T(8,128)(2,1)} %get-tuple-element.7) | data formatting | bytes 163840 | tf_op jit(solution)/shard_map/reshape | solution.py:372
  49.1 0.7 %fusion = (bf16[1,4,4,2,640]{4,1,0,3,2:T(4,128)(2,1)}, bf16[1,4,4,2,640]{4,1,0,3,2:T(4,128)(2,1)}) fusion(bf16[2,4,4,2,640]{4,1,0,3,2:T(4,128)(2,1)S(1)} %bitcast.14), kind=kLoop, calls=%fused_computation.2 | loop fusion | bytes 163840 | tf_op jit(solution)/shard_map/slice | solution.py:374
  49.8 0.0 copy-start
  49.8 2.5 %copy.19 = f32[1,2,1280,128]{3,2,1,0:T(8,128)} copy(f32[1,2,1280,128]{3,2,1,0:T(8,128)} %bitcast.10) | data formatting | bytes 2621440
  52.3 0.0 copy-done
  52.3 0.8 %copy.20 = f32[1,1280,128]{2,1,0:T(8,128)} copy(f32[1,1280,128]{2,1,0:T(8,128)S(1)} %bitcast.12) | data formatting | bytes 1310720
  (2 shorter events, 0.1 us)
Async XLA Ops:
  49.8 2.5 %copy-start = (f32[1280,128]{1,0:T(8,128)S(1)}, f32[1280,128]{1,0:T(8,128)}, u32[]{:S(2)}) copy-start(f32[1280,128]{1,0:T(8,128)} %get-tuple-element.9) | copy-start | bytes 1966084

commit v3 on v2

v3 whole, which is shorter than its diff:
```python
import functools

import jax
import jax.numpy as jnp
import numpy as np
from jax import lax
from jax.experimental import pallas as pl
from jax.experimental.pallas import tpu as pltpu
from jax.sharding import PartitionSpec as P

MESH = pl.DeviceIdType.MESH
BF16 = jnp.bfloat16
F32 = jnp.float32
PAIR = 2


def dot(a, b, contract):
    return lax.dot_general(a, b, ((contract[:1], contract[1:]), ((), ())), preferred_element_type=F32)


def kernel(
    dims,
    tokens_ref, cotangent_ref, dest_ref, counts_ref, placement_ref, gate_up_ref, down_ref,
    rows_out, grads_out,
    inbox, metas, xall, weights, part_gu, part_h, in_gu, in_h, hidden, grads, outrows, mine, yin, zin, own, outbox, inbox2, acc,
    pack_sems, meta_sems, up_sems, down_sems, y_sems, part_sems, grad_sems, yo_sems, zo_sems, out_sems, w_sems, o_sems,
):
    groups, zs, fold, tok, experts, split, per_dot = dims
    me, ep = lax.axis_index("grp"), lax.axis_index("ep")
    z, y = ep // PAIR, ep % PAIR
    other = z * PAIR + (PAIR - 1 - y)
    width, slc = xall.shape[-1], hidden.shape[-1]
    cols, box = outbox.shape[-1], outbox.shape[1]
    rows = xall.shape[3]
    block, cap = tok // groups, tok // experts
    blocks = PAIR * zs
    share = blocks // groups
    n_in, n_rows = groups * 2 * tok, 2 * rows

    grp_peers = [(d, lax.rem(me + d, groups)) for d in range(1, groups)]
    z_peers = [(d, lax.rem(z + d, zs)) for d in range(1, zs)]

    barrier = pltpu.get_barrier_semaphore()
    for _, p in grp_peers:
        pl.semaphore_signal(barrier, inc=1, device_id=(p, ep), device_id_type=MESH)
    for _, q in z_peers:
        pl.semaphore_signal(barrier, inc=1, device_id=(me, q * PAIR + y), device_id_type=MESH)
    pl.semaphore_signal(barrier, inc=1, device_id=(me, other), device_id_type=MESH)

    def piece(ref, p):
        if ref.shape[0] == 1:
            return ref.at[0, :, pl.ds(pl.multiple_of(p * width, width), width)]
        return ref.at[p]

    loads = [
        pltpu.make_async_copy(piece(tokens_ref, me), inbox.at[me, 0], w_sems.at[3]),
        pltpu.make_async_copy(piece(cotangent_ref, me), inbox.at[me, 1], w_sems.at[4]),
        pltpu.make_async_copy(gate_up_ref.at[0], weights.at[:, pl.ds(0, slc)], w_sems.at[0]),
        pltpu.make_async_copy(gate_up_ref.at[1], weights.at[:, pl.ds(slc, slc)], w_sems.at[1]),
        pltpu.make_async_copy(down_ref, weights.at[:, pl.ds(2 * slc, slc)], w_sems.at[2]),
    ]
    for load in loads:
        load.start()

    lanes = metas.shape[-1]
    lane = lax.broadcasted_iota(jnp.int32, (8, lanes), 1)
    line = lax.broadcasted_iota(jnp.int32, (8, lanes), 0)

    def slots(group, row):
        return group * block + lax.rem(row, block)

    lane_row, lane_group = lax.rem(lane, tok), lax.rem(lax.div(lane, tok), groups)
    lane_block = lax.div(lane_row, block)
    lane_expert = lax.div(slots(lane_group, lane_row), cap)
    own_dest = sum(jnp.where(lane_block == b, dest_ref[0, 0, b], 0) for b in range(groups))
    own_count = sum(jnp.where(lane_expert == e, counts_ref[0, 0, e], 0) for e in range(experts))
    metas[me] = jnp.where(line == 0, own_dest, own_count)

    pl.semaphore_wait(barrier, groups - 1 + zs - 1 + 1)

    def remote(src, dst, sems, at, device):
        return pltpu.make_async_remote_copy(
            src_ref=src, dst_ref=dst, send_sem=sems.at[0, at], recv_sem=sems.at[1, at],
            device_id=device, device_id_type=MESH,
        )

    sent = []

    meta_copies = [remote(metas.at[me], metas.at[me], meta_sems, d, (p, ep)) for d, p in grp_peers]
    pack_copies = [
        [
            remote(piece(ref, p), inbox.at[me, t], pack_sems, t * groups + d, (p, ep))
            for d, p in grp_peers
        ]
        for t, ref in enumerate((tokens_ref, cotangent_ref))
    ]
    for copy in meta_copies + pack_copies[0] + pack_copies[1]:
        copy.start()
    sent += meta_copies + pack_copies[0] + pack_copies[1]

    m = lax.broadcasted_iota(jnp.int32, (1, n_rows), 1)
    m_kind, m_group, m_row = lax.div(m, rows), lax.rem(lax.div(m, tok), groups), lax.rem(m, tok)
    slot = slots(m_group, m_row)
    base = m_kind * tok + slot
    out_at = lax.broadcasted_iota(jnp.int32, (groups * box, n_rows), 0)
    row_at = lax.broadcasted_iota(jnp.int32, (rows, tok), 0)
    col_at = lax.broadcasted_iota(jnp.int32, (rows, tok), 1)

    for copy in meta_copies:
        copy.wait_recv()
    dest = sum(jnp.where(m_group == g, metas[g, 0:1, 0:n_rows], 0) for g in range(groups))
    kept = sum(
        jnp.where((dest == h) & (lax.rem(slot, cap) < metas[h, 1:2, 0:n_rows]), 1, 0)
        for h in range(groups)
    )

    def own_rows(t):
        loads[t].wait()
        for copy in pack_copies[t]:
            copy.wait_recv()
        picked = jnp.zeros((rows, width), F32)
        for g in range(groups):
            keep = kept[:, g * tok:(g + 1) * tok]
            place = jnp.where((row_at == g * tok + col_at) & (keep > 0), 1.0, 0.0).astype(BF16)
            picked = picked + dot(place, inbox[g, t], (1, 0))
        xall[0, z, t] = picked.astype(BF16)

    def to_other(t, at, source):
        return remote(xall.at[0, source, t], xall.at[1, source, t], y_sems, t * 2 * zs + at, (me, other))

    def up(t, hop, source):
        return remote(
            xall.at[0, source, t], xall.at[0, source, t], up_sems, t * zs + hop, (me, (z + 1) * PAIR + y)
        )

    def down(t, hop, source):
        return remote(
            xall.at[0, source, t], xall.at[0, source, t], down_sems, t * zs + hop, (me, (z - 1) * PAIR + y)
        )

    def send_own(t):
        pl.when(z < zs - 1)(lambda: up(t, 1, z).start())
        pl.when(z > 0)(lambda: down(t, 1, z).start())
        to_other(t, 0, z).start()

    def pass_on(t):
        for hop in range(1, zs):
            @pl.when(z >= hop)
            def _(hop=hop):
                up(t, hop, z - hop).wait_recv()
                if hop < zs - 1:
                    pl.when(z < zs - 1)(lambda: up(t, hop + 1, z - hop).start())
                to_other(t, hop, z - hop).start()

            @pl.when(z + hop < zs)
            def _(hop=hop):
                down(t, hop, z + hop).wait_recv()
                if hop < zs - 1:
                    pl.when(z > 0)(lambda: down(t, hop + 1, z + hop).start())
                to_other(t, zs + hop, z + hop).start()

    def arrivals(t, wait):
        wait(to_other(t, 0, z))
        for hop in range(1, zs):
            pl.when(z >= hop)(lambda: wait(to_other(t, hop, z - hop)))
            pl.when(z + hop < zs)(lambda: wait(to_other(t, zs + hop, z + hop)))

    def passed(t):
        for hop in range(1, zs):
            pl.when((z < zs - 1) & (z >= hop - 1))(lambda: up(t, hop, z - hop + 1).wait_send())
            pl.when((z > 0) & (z + hop - 1 < zs))(lambda: down(t, hop, z + hop - 1).wait_send())
        arrivals(t, lambda copy: copy.wait_send())

    def x_rows(side, first, kind):
        return xall[side, pl.ds(first, per_dot), kind].reshape(per_dot * rows, width)

    def each(body):
        def step(i, carry):
            body(i * per_dot)
            return carry

        lax.fori_loop(0, zs // per_dot, step, 0)

    def project(side, kind, low, high, target):
        def step(first):
            out = dot(x_rows(side, first, kind), weights[:, low * slc:high * slc], (1, 0))
            target[pl.ds(side * zs + first, per_dot)] = (
                out.astype(BF16).reshape(per_dot, rows, (high - low) * slc)
            )

        each(step)

    def send_parts(t, source, target):
        copies = [
            remote(source.at[pl.ds(p * share, share)], target.at[me], part_sems, t * groups + d, (p, ep))
            for d, p in grp_peers
        ]
        for copy in copies:
            copy.start()
        return copies

    held = pl.ds(me * share, share)

    def summed(copies, source, target):
        total = source[held].astype(F32)
        for d, copy in zip(range(1, groups), copies):
            copy.wait_recv()
            total = total + target[lax.rem(me + groups - d, groups)].astype(F32)
        return total

    def share_out(t, ref):
        copies = [
            remote(ref.at[held], ref.at[held], grad_sems, t * groups + d, (p, ep))
            for d, p in grp_peers
        ]
        for copy in copies:
            copy.start()
        return copies

    def only_served(value):
        if experts == 1:
            return value
        row = lax.broadcasted_iota(jnp.int32, value.shape, 1)
        expert = lax.div(slots(lax.div(row, tok), lax.rem(row, tok)), cap)
        return jnp.where(expert == lax.div(placement_ref[ep], split), value, 0.0)

    def rows_of(ref, side, first):
        return ref[pl.ds(side * zs + first, per_dot)].reshape(per_dot * rows, ref.shape[-1])

    def produce(side, kind, target):
        def step(first):
            source, low, high = ((hidden, 2, 3), (grads, 0, 2))[kind]
            out = dot(rows_of(source, side, first), weights[:, low * slc:high * slc], (1, 1))
            target[pl.ds(first, per_dot), kind] = out.astype(target.dtype).reshape(per_dot, rows, width)

        each(step)

    order = [lax.rem(z + d, zs) for d in list(range(1, zs)) + [0]]

    def send_across(t):
        copies = [
            remote(outrows.at[q, t], yin.at[q, t], yo_sems, t * zs + i, (me, other))
            for i, q in enumerate(order)
        ]
        for copy in copies:
            copy.start()
        return copies

    def send_along(t, copies):
        out = []
        for i, q in enumerate(order):
            copies[i].wait()
            total = mine[q, t].astype(F32) + yin[q, t].astype(F32)
            if i < zs - 1:
                outrows[q, t] = total.astype(BF16)
                copy = remote(
                    outrows.at[q, t], zin.at[z, t], zo_sems, t * zs + i + 1, (me, q * PAIR + y)
                )
                copy.start()
                out.append(copy)
            else:
                own[t] = total
        return out

    for t in range(2):
        own_rows(t)
        send_own(t)
    pass_on(0)
    for load in loads[2:]:
        load.wait()
    project(0, 0, 0, 2, part_gu)
    pass_on(1)
    arrivals(0, lambda copy: copy.wait_recv())
    project(1, 0, 0, 2, part_gu)
    gu_copies = send_parts(0, part_gu, in_gu)
    project(0, 1, 2, 3, part_h)

    gate_up = summed(gu_copies, part_gu, in_gu)
    gate, up_part = gate_up[:, :, 0:slc], gate_up[:, :, slc:2 * slc]
    sig = jax.nn.sigmoid(gate)
    activated = gate * sig
    hidden[held] = only_served(activated * up_part).astype(BF16)
    hidden_copies = share_out(0, hidden)

    arrivals(1, lambda copy: copy.wait_recv())
    project(1, 1, 2, 3, part_h)
    h_copies = send_parts(1, part_h, in_h)

    for copy in hidden_copies:
        copy.wait_recv()
    produce(1, 0, outrows)
    across_ahead = send_across(0)
    produce(0, 0, mine)

    hidden_grad = summed(h_copies, part_h, in_h)
    gate_grad = hidden_grad * up_part * sig * (1.0 + gate * (1.0 - sig))
    grads[held, :, 0:slc] = only_served(gate_grad).astype(BF16)
    grads[held, :, slc:2 * slc] = only_served(hidden_grad * activated).astype(BF16)
    grad_copies = share_out(1, grads)

    along_ahead = send_along(0, across_ahead)

    for copy in grad_copies:
        copy.wait_recv()
    produce(1, 1, outrows)
    across_back = send_across(1)
    produce(0, 1, mine)
    along_back = send_along(1, across_back)

    if blocks == PAIR * per_dot:
        def both_sides(ref):
            return ref[...].reshape(blocks * rows, ref.shape[-1])

        def all_rows(kind):
            return xall[:, :, kind].reshape(blocks * rows, width)

        acc[:, 0:2 * slc] = dot(all_rows(0), both_sides(grads), (0, 0))
        acc[:, 2 * slc:3 * slc] = dot(all_rows(1), both_sides(hidden), (0, 0))
    else:
        acc[...] = jnp.zeros_like(acc)
        for side in range(PAIR):
            def step(first, side=side):
                acc[:, 0:2 * slc] += dot(x_rows(side, first, 0), rows_of(grads, side, first), (0, 0))
                acc[:, 2 * slc:3 * slc] += dot(x_rows(side, first, 1), rows_of(hidden, side, first), (0, 0))

            each(step)
    for i in range(3):
        grads_out[i] = acc[:, i * slc:(i + 1) * slc].astype(grads_out.dtype)

    target = dest * (fold * 2 * tok) + base
    picks = [
        jnp.where(out_at == target + f * 2 * tok, 1.0, 0.0).astype(BF16) for f in range(fold)
    ]
    for t, copies in enumerate((along_ahead, along_back)):
        for d, copy in zip(range(1, zs), copies):
            copy.wait_recv()
            own[t] += zin[lax.rem(z + zs - d, zs), t].astype(F32)

    final = own[...].astype(BF16).reshape(n_rows, width)
    placed = sum(dot(picks[f], final[:, f * cols:(f + 1) * cols], (1, 0)) for f in range(fold))
    outbox[...] = placed.astype(BF16).reshape(outbox.shape)
    out_copies = [remote(outbox.at[p], inbox2.at[me], out_sems, d, (p, ep)) for d, p in grp_peers]
    for copy in out_copies:
        copy.start()
    sent += out_copies + along_ahead + along_back + gu_copies + h_copies + hidden_copies + grad_copies
    inbox2[me] = outbox[me]
    for copy in out_copies:
        copy.wait_recv()
    rows_out[...] = inbox2[...]
    for copy in sent:
        copy.wait_send()
    passed(0)
    passed(1)


def body(tokens, cotangent, counts, destination, placement, gate_up_weight, down_weight):
    groups = lax.axis_size("grp")
    owners = lax.axis_size("ep")
    tok, model = tokens.shape[1], tokens.shape[2]
    experts = counts.shape[2]
    split = owners // experts
    width, slc = down_weight.shape[1], down_weight.shape[2]
    zs = owners // PAIR
    fold = max(1, 16 // (2 * tok))
    cols = width // fold
    box = fold * 2 * tok
    rows = groups * tok
    per_dot = min(zs, max(1, 64 // rows))
    lanes = -(-2 * rows // 128) * 128
    if width % 128:
        tokens, cotangent = (
            jnp.transpose(v[0].reshape(tok, groups, width), (1, 0, 2)) for v in (tokens, cotangent)
        )

    blocks = PAIR * zs
    share = blocks // groups
    vmem = pl.BlockSpec(memory_space=pltpu.VMEM)
    smem = pl.BlockSpec(memory_space=pltpu.SMEM)
    anywhere = pl.BlockSpec(memory_space=pl.ANY)
    shapes = [
        ((groups, 2, tok, width), BF16),
        ((groups, 8, lanes), jnp.int32),
        ((PAIR, zs, 2, rows, width), BF16),
        ((width, 3 * slc), BF16),
        ((blocks, rows, 2 * slc), BF16),
        ((blocks, rows, slc), BF16),
        ((groups, share, rows, 2 * slc), BF16),
        ((groups, share, rows, slc), BF16),
        ((blocks, rows, slc), BF16),
        ((blocks, rows, 2 * slc), BF16),
        ((zs, 2, rows, width), BF16),
        ((zs, 2, rows, width), F32 if zs * rows * width < (1 << 20) else BF16),
        ((zs, 2, rows, width), BF16),
        ((zs, 2, rows, width), BF16),
        ((2, rows, width), F32),
        ((groups, box, cols), BF16),
        ((groups, box, cols), BF16),
        ((width, 3 * slc), F32),
    ]
    dma = pltpu.SemaphoreType.DMA
    out, grads = pl.pallas_call(
        functools.partial(kernel, (groups, zs, fold, tok, experts, split, per_dot)),
        out_shape=(
            jax.ShapeDtypeStruct((groups, box, cols), BF16),
            jax.ShapeDtypeStruct((3, width, slc), BF16),
        ),
        in_specs=[anywhere, anywhere, smem, smem, smem, anywhere, anywhere],
        out_specs=(vmem, vmem),
        scratch_shapes=[pltpu.VMEM(s, t) for s, t in shapes] + [
            dma((2, 2 * groups)), dma((2, groups)), dma((2, 2 * zs)), dma((2, 2 * zs)), dma((2, 4 * zs)),
            dma((2, 2 * groups)), dma((2, 2 * groups)), dma((2, 2 * zs)), dma((2, 2 * zs)), dma((2, groups)),
            dma((5,)), dma((2,)),
        ],
        compiler_params=pltpu.CompilerParams(
            collective_id=0, has_side_effects=True, vmem_limit_bytes=60 << 20
        ),
    )(tokens, cotangent, destination, counts, placement, gate_up_weight[0], down_weight[0])
    out = out.reshape(groups, fold, 2, tok, cols)
    out = jnp.transpose(out, (2, 3, 0, 1, 4)).reshape(2, 1, tok, model)
    grads = grads.astype(F32)
    return out[0], out[1], grads[None, 0:2], grads[2:3]


def solution(mesh):
    return jax.shard_map(
        body,
        mesh=mesh,
        in_specs=(
            P("grp", "ep", None),
            P("grp", "ep", None),
            P("grp", "ep", None),
            P("grp", "ep", None),
            P(),
            P("ep", None, "grp", None),
            P("ep", "grp", None),
        ),
        out_specs=(
            P("grp", "ep", None),
            P("grp", "ep", None),
            P("ep", None, "grp", None),
            P("ep", "grp", None),
        ),
        check_vma=False,
    )
```

time: 53.4 us -> 52.8 us (0.989)
  Pallas kernels: 45.3 us -> 46.5 us
  local copies, waits for them, and re-layouts: 5.66 us -> 4.65 us
  other arithmetic: 0.86 us -> 0.13 us
    unnamed x4 -> x2, local copies, waits for them, and re-layouts: 3.36 us -> 0.01 us
    slice x1 -> x2, local copies, waits for them, and re-layouts: 0.66 us -> 2.51 us  [body(): return (out[0], out[1], grads[None, 0:2], grads[2:3])]
    pallas_call x1, Pallas kernels: 45.3 us -> 46.5 us  [body(): pl.pallas_call(functools.partial(kernel, (groups, zs, fold, tok, experts,...]
    broadcast_in_dim x0 -> x1, local copies, waits for them, and re-layouts: none -> 1.14 us  [body(): return (out[0], out[1], grads[None, 0:2], grads[2:3])]
    another operation x1 -> x0, other arithmetic: 0.86 us -> none  [body(): jnp.stack([tokens[0], cotangent[0]]).reshape(2, tok, groups, fold, cols)]
    reshape x3 -> x0, local copies, waits for them, and re-layouts: 0.73 us -> none  [the longest x1 0.66 us: body(): packed = jnp.transpose(packed, (2, 3, 0, 1, 4)).reshape(groups, box, cols)]
where the time goes in v3:
time: 52.8 us; the launch traced here: 52.6 us
  Pallas kernels  46.5 us (88%)
  local copies, waits for them, and re-layouts  4.65 us (9%)
  between operations  1.3 us (2%)
    pallas_call x1, Pallas kernels, body(): pl.pallas_call(functools.partial(kernel, (groups, zs, fold, tok, experts,...  46.5 us
    slice x2, local copies, waits for them, and re-layouts, body(): return (out[0], out[1], grads[None, 0:2], grads[2:3])  2.51 us
    broadcast_in_dim x1, local copies, waits for them, and re-layouts, body(): return (out[0], out[1], grads[None, 0:2], grads[2:3])  1.14 us

profile of v3, /device:TPU:0, one launch (start us, length us, event | category | flops | bytes accessed | tf_op | source)
XLA Modules:
  0.0 52.6 jit_solution(2590943564996034866)
XLA Ops:
  1.3 46.5 %shard_map.102 = (bf16[4,16,640]{2,1,0:T(8,128)(2,1)}, bf16[3,1280,128]{2,1,0:T(8,128)(2,1)}) custom-call(bf16[1,4,5120]{2,1,0:T(4,128)(2,1)} %tokens_ref.1, bf16[1,4,5120]{2,1,0:T(4,128)(2,1)} %cotangent_ref.1, s32[1,1,4]{2,1,0:T(1,128)} %dest_ref.1, s32[1,1,1]{2,1,0:T(1,128)S(6)} %copy.13.counts_ref, s32[8]{0:T(128)} %placement_ref.1, ...), custom_call_target="tpu_custom_call" | custom-call | tf_op jit(solution)/shard_map/pallas_call | solution.py:401
  47.8 0.0 copy-start
  47.8 1.0 %reshape.16 = bf16[4,2,2,4,640]{4,3,2,1,0:T(4,128)(2,1)S(1)} reshape(bf16[4,16,640]{2,1,0:T(8,128)(2,1)} %get-tuple-element.6) | data formatting | bytes 163840 | tf_op jit(solution)/shard_map/reshape | solution.py:418
  48.8 0.7 %fusion = (bf16[1,4,4,2,640]{4,1,0,3,2:T(4,128)(2,1)}, bf16[1,4,4,2,640]{4,1,0,3,2:T(4,128)(2,1)}) fusion(bf16[2,4,4,2,640]{4,1,0,3,2:T(4,128)(2,1)S(1)} %bitcast.9), kind=kLoop, calls=%fused_computation.1 | loop fusion | bytes 163840 | tf_op jit(solution)/shard_map/slice | solution.py:421
  49.4 1.9 %slice.21 = f32[1,1280,128]{2,1,0:T(8,128)} slice(bf16[3,1280,128]{2,1,0:T(8,128)(2,1)} %get-tuple-element.7), slice={[2:3], [0:1280], [0:128]} | slice | bytes 1310720 | tf_op jit(solution)/shard_map/slice | solution.py:421
  51.3 0.0 copy-done
  51.3 0.1 convert_element_type.3
  51.4 1.1 %slice_bitcast_fusion = f32[1,2,1280,128]{3,2,1,0:T(8,128)} fusion(f32[3,1280,128]{2,1,0:T(8,128)S(1)} %convert_element_type.3), kind=kLoop, calls=%fused_computation | loop fusion | bytes 2621440 | tf_op jit(solution)/shard_map/broadcast_in_dim | solution.py:421
Async XLA Ops:
  47.8 3.5 %copy-start = (bf16[3,1280,128]{2,1,0:T(8,128)(2,1)S(1)}, bf16[3,1280,128]{2,1,0:T(8,128)(2,1)}, u32[]{:S(2)}) copy-start(bf16[3,1280,128]{2,1,0:T(8,128)(2,1)} %get-tuple-element.7) | copy-start | bytes 2949124

commit v4 on v3

--- a/solution.py
+++ b/solution.py
@@ -21,30 +21,47 @@
 def kernel(
     dims,
     tokens_ref, cotangent_ref, dest_ref, counts_ref, placement_ref, gate_up_ref, down_ref,
-    rows_out, grads_out,
-    inbox, metas, xall, weights, part_gu, part_h, in_gu, in_h, hidden, grads, outrows, mine, yin, zin, own, outbox, inbox2, acc,
-    pack_sems, meta_sems, up_sems, down_sems, y_sems, part_sems, grad_sems, yo_sems, zo_sems, out_sems, w_sems, o_sems,
+    rows_out, gate_up_out, down_out,
+    inbox, metas, dests, xall, weights, part_gu, part_h, in_gu, in_h, hidden, grads, outrows, mine, yin, placed, zin, acc,
+    pack_sems, meta_sems, dest_sems, z_sems, y_sems, part_sems, grad_sems, yo_sems, zo_sems, w_sems,
 ):
-    groups, zs, fold, tok, experts, split, per_dot = dims
+    groups, zs, tok, experts, split, per_dot = dims
+    if len(outrows.shape) == 5:
+        placed = outrows
     me, ep = lax.axis_index("grp"), lax.axis_index("ep")
     z, y = ep // PAIR, ep % PAIR
     other = z * PAIR + (PAIR - 1 - y)
     width, slc = xall.shape[-1], hidden.shape[-1]
-    cols, box = outbox.shape[-1], outbox.shape[1]
     rows = xall.shape[3]
     block, cap = tok // groups, tok // experts
     blocks = PAIR * zs
     share = blocks // groups
-    n_in, n_rows = groups * 2 * tok, 2 * rows
+    n_rows = 2 * rows
 
     grp_peers = [(d, lax.rem(me + d, groups)) for d in range(1, groups)]
     z_peers = [(d, lax.rem(z + d, zs)) for d in range(1, zs)]
 
+    def for_groups(first, body):
+        if groups <= 8:
+            for d in range(first, groups):
+                body(d)
+        else:
+            def step(d, carry):
+                body(d)
+                return carry
+
+            lax.fori_loop(first, groups, step, 0)
+
+    order = [(i, lax.rem(z + i + 1, zs)) for i in range(zs)]
+
     barrier = pltpu.get_barrier_semaphore()
-    for _, p in grp_peers:
-        pl.semaphore_signal(barrier, inc=1, device_id=(p, ep), device_id_type=MESH)
-    for _, q in z_peers:
-        pl.semaphore_signal(barrier, inc=1, device_id=(me, q * PAIR + y), device_id_type=MESH)
+    for i, q in order:
+        def greet(d, q=q):
+            pl.semaphore_signal(
+                barrier, inc=1, device_id=(lax.rem(me + d, groups), q * PAIR + y), device_id_type=MESH
+            )
+
+        for_groups(1 if i == zs - 1 else 0, greet)
     pl.semaphore_signal(barrier, inc=1, device_id=(me, other), device_id_type=MESH)
 
     def piece(ref, p):
@@ -76,7 +93,7 @@
     own_count = sum(jnp.where(lane_expert == e, counts_ref[0, 0, e], 0) for e in range(experts))
     metas[me] = jnp.where(line == 0, own_dest, own_count)
 
-    pl.semaphore_wait(barrier, groups - 1 + zs - 1 + 1)
+    pl.semaphore_wait(barrier, groups * zs)
 
     def remote(src, dst, sems, at, device):
         return pltpu.make_async_remote_copy(
@@ -99,10 +116,8 @@
     sent += meta_copies + pack_copies[0] + pack_copies[1]
 
     m = lax.broadcasted_iota(jnp.int32, (1, n_rows), 1)
-    m_kind, m_group, m_row = lax.div(m, rows), lax.rem(lax.div(m, tok), groups), lax.rem(m, tok)
+    m_group, m_row = lax.rem(lax.div(m, tok), groups), lax.rem(m, tok)
     slot = slots(m_group, m_row)
-    base = m_kind * tok + slot
-    out_at = lax.broadcasted_iota(jnp.int32, (groups * box, n_rows), 0)
     row_at = lax.broadcasted_iota(jnp.int32, (rows, tok), 0)
     col_at = lax.broadcasted_iota(jnp.int32, (rows, tok), 1)
 
@@ -113,6 +128,11 @@
         jnp.where((dest == h) & (lax.rem(slot, cap) < metas[h, 1:2, 0:n_rows]), 1, 0)
         for h in range(groups)
     )
+    dests[z, :, 0:n_rows] = jnp.broadcast_to(dest, (8, n_rows))
+    dest_copies = [remote(dests.at[z], dests.at[z], dest_sems, d, (me, q * PAIR + y)) for d, q in z_peers]
+    for copy in dest_copies:
+        copy.start()
+    sent += dest_copies
 
     def own_rows(t):
         loads[t].wait()
@@ -126,50 +146,32 @@
         xall[0, z, t] = picked.astype(BF16)
 
     def to_other(t, at, source):
-        return remote(xall.at[0, source, t], xall.at[1, source, t], y_sems, t * 2 * zs + at, (me, other))
-
-    def up(t, hop, source):
+        return remote(xall.at[0, source, t], xall.at[1, source, t], y_sems, t * zs + at, (me, other))
+
+    def along(t, d):
         return remote(
-            xall.at[0, source, t], xall.at[0, source, t], up_sems, t * zs + hop, (me, (z + 1) * PAIR + y)
+            xall.at[0, z, t], xall.at[0, z, t], z_sems, t * zs + d, (me, lax.rem(z + d, zs) * PAIR + y)
         )
 
-    def down(t, hop, source):
-        return remote(
-            xall.at[0, source, t], xall.at[0, source, t], down_sems, t * zs + hop, (me, (z - 1) * PAIR + y)
-        )
-
     def send_own(t):
-        pl.when(z < zs - 1)(lambda: up(t, 1, z).start())
-        pl.when(z > 0)(lambda: down(t, 1, z).start())
         to_other(t, 0, z).start()
+        for d in range(1, zs):
+            along(t, d).start()
 
     def pass_on(t):
-        for hop in range(1, zs):
-            @pl.when(z >= hop)
-            def _(hop=hop):
-                up(t, hop, z - hop).wait_recv()
-                if hop < zs - 1:
-                    pl.when(z < zs - 1)(lambda: up(t, hop + 1, z - hop).start())
-                to_other(t, hop, z - hop).start()
-
-            @pl.when(z + hop < zs)
-            def _(hop=hop):
-                down(t, hop, z + hop).wait_recv()
-                if hop < zs - 1:
-                    pl.when(z > 0)(lambda: down(t, hop + 1, z + hop).start())
-                to_other(t, zs + hop, z + hop).start()
-
-    def arrivals(t, wait):
-        wait(to_other(t, 0, z))
-        for hop in range(1, zs):
-            pl.when(z >= hop)(lambda: wait(to_other(t, hop, z - hop)))
-            pl.when(z + hop < zs)(lambda: wait(to_other(t, zs + hop, z + hop)))
+        for d in range(1, zs):
+            along(t, d).wait_recv()
+            to_other(t, d, lax.rem(z + zs - d, zs)).start()
+
+    def arrivals(t):
+        for d in range(zs):
+            to_other(t, d, lax.rem(z + zs - d, zs)).wait_recv()
 
     def passed(t):
-        for hop in range(1, zs):
-            pl.when((z < zs - 1) & (z >= hop - 1))(lambda: up(t, hop, z - hop + 1).wait_send())
-            pl.when((z > 0) & (z + hop - 1 < zs))(lambda: down(t, hop, z + hop - 1).wait_send())
-        arrivals(t, lambda copy: copy.wait_send())
+        for d in range(zs):
+            if d > 0:
+                along(t, d).wait_send()
+            to_other(t, d, lax.rem(z + zs - d, zs)).wait_send()
 
     def x_rows(side, first, kind):
         return xall[side, pl.ds(first, per_dot), kind].reshape(per_dot * rows, width)
@@ -231,36 +233,48 @@
         def step(first):
             source, low, high = ((hidden, 2, 3), (grads, 0, 2))[kind]
             out = dot(rows_of(source, side, first), weights[:, low * slc:high * slc], (1, 1))
-            target[pl.ds(first, per_dot), kind] = out.astype(target.dtype).reshape(per_dot, rows, width)
+            target[pl.ds(first, per_dot), kind] = out.astype(target.dtype).reshape((per_dot,) + target.shape[2:])
 
         each(step)
-
-    order = [lax.rem(z + d, zs) for d in list(range(1, zs)) + [0]]
 
     def send_across(t):
         copies = [
-            remote(outrows.at[q, t], yin.at[q, t], yo_sems, t * zs + i, (me, other))
-            for i, q in enumerate(order)
+            remote(outrows.at[q, t], yin.at[q, t], yo_sems, t * zs + i, (me, other)) for i, q in order
         ]
         for copy in copies:
             copy.start()
         return copies
 
-    def send_along(t, copies):
-        out = []
-        for i, q in enumerate(order):
+    def deliver(t, i, q, d):
+        p = lax.rem(me + d, groups)
+        return remote(
+            placed.at[q, t, p], zin.at[z, me, t], zo_sems, (t * zs + i) * groups + d, (p, q * PAIR + y)
+        )
+
+    slot_at = lax.broadcasted_iota(jnp.int32, (tok, rows), 0)
+
+    def send_home(t, copies):
+        for i, q in order:
             copies[i].wait()
-            total = mine[q, t].astype(F32) + yin[q, t].astype(F32)
-            if i < zs - 1:
-                outrows[q, t] = total.astype(BF16)
-                copy = remote(
-                    outrows.at[q, t], zin.at[z, t], zo_sems, t * zs + i + 1, (me, q * PAIR + y)
-                )
-                copy.start()
-                out.append(copy)
-            else:
-                own[t] = total
-        return out
+            total = (mine[q, t].astype(F32) + yin[q, t].reshape(rows, width).astype(F32)).astype(BF16)
+            going = dests[q, 0:1, 0:rows]
+
+            def place(p):
+                pick = jnp.where((slot_at == slot[:, 0:rows]) & (going == p), 1.0, 0.0).astype(BF16)
+                return dot(pick, total, (1, 0)).astype(BF16)
+
+            def send(d, i=i, q=q, place=place):
+                p = lax.rem(me + d, groups)
+                placed[q, t, p] = place(p)
+                deliver(t, i, q, d).start()
+
+            for_groups(1 if i == zs - 1 else 0, send)
+            if i == zs - 1:
+                zin[z, me, t] = place(me)
+
+    def delivered(t, wait):
+        for i, q in order:
+            for_groups(1 if i == zs - 1 else 0, lambda d, i=i, q=q: wait(deliver(t, i, q, d)))
 
     for t in range(2):
         own_rows(t)
@@ -270,7 +284,7 @@
         load.wait()
     project(0, 0, 0, 2, part_gu)
     pass_on(1)
-    arrivals(0, lambda copy: copy.wait_recv())
+    arrivals(0)
     project(1, 0, 0, 2, part_gu)
     gu_copies = send_parts(0, part_gu, in_gu)
     project(0, 1, 2, 3, part_h)
@@ -282,7 +296,7 @@
     hidden[held] = only_served(activated * up_part).astype(BF16)
     hidden_copies = share_out(0, hidden)
 
-    arrivals(1, lambda copy: copy.wait_recv())
+    arrivals(1)
     project(1, 1, 2, 3, part_h)
     h_copies = send_parts(1, part_h, in_h)
 
@@ -298,14 +312,16 @@
     grads[held, :, slc:2 * slc] = only_served(hidden_grad * activated).astype(BF16)
     grad_copies = share_out(1, grads)
 
-    along_ahead = send_along(0, across_ahead)
+    for copy in dest_copies:
+        copy.wait_recv()
+    send_home(0, across_ahead)
 
     for copy in grad_copies:
         copy.wait_recv()
     produce(1, 1, outrows)
     across_back = send_across(1)
     produce(0, 1, mine)
-    along_back = send_along(1, across_back)
+    send_home(1, across_back)
 
     if blocks == PAIR * per_dot:
         def both_sides(ref):
@@ -324,33 +340,27 @@
                 acc[:, 2 * slc:3 * slc] += dot(x_rows(side, first, 1), rows_of(hidden, side, first), (0, 0))
 
             each(step)
-    for i in range(3):
-        grads_out[i] = acc[:, i * slc:(i + 1) * slc].astype(grads_out.dtype)
-
-    target = dest * (fold * 2 * tok) + base
-    picks = [
-        jnp.where(out_at == target + f * 2 * tok, 1.0, 0.0).astype(BF16) for f in range(fold)
-    ]
-    for t, copies in enumerate((along_ahead, along_back)):
-        for d, copy in zip(range(1, zs), copies):
-            copy.wait_recv()
-            own[t] += zin[lax.rem(z + zs - d, zs), t].astype(F32)
-
-    final = own[...].astype(BF16).reshape(n_rows, width)
-    placed = sum(dot(picks[f], final[:, f * cols:(f + 1) * cols], (1, 0)) for f in range(fold))
-    outbox[...] = placed.astype(BF16).reshape(outbox.shape)
-    out_copies = [remote(outbox.at[p], inbox2.at[me], out_sems, d, (p, ep)) for d, p in grp_peers]
-    for copy in out_copies:
-        copy.start()
-    sent += out_copies + along_ahead + along_back + gu_copies + h_copies + hidden_copies + grad_copies
-    inbox2[me] = outbox[me]
-    for copy in out_copies:
-        copy.wait_recv()
-    rows_out[...] = inbox2[...]
+    for i in range(2):
+        gate_up_out[i] = acc[:, i * slc:(i + 1) * slc].astype(gate_up_out.dtype)
+    down_out[...] = acc[:, 2 * slc:3 * slc].astype(down_out.dtype)
+
+    for t in range(2):
+        delivered(t, lambda copy: copy.wait_recv())
+        for g in range(groups):
+            total = zin[0, g, t].astype(F32)
+            for q in range(1, zs):
+                total = total + zin[q, g, t].astype(F32)
+            total = total.astype(BF16)
+            if rows_out.shape[0] == 2:
+                rows_out[t, :, g * width:(g + 1) * width] = total
+            else:
+                rows_out[g, t] = total
+    sent += gu_copies + h_copies + hidden_copies + grad_copies
     for copy in sent:
         copy.wait_send()
-    passed(0)
-    passed(1)
+    for t in range(2):
+        passed(t)
+        delivered(t, lambda copy: copy.wait_send())
 
 
 def body(tokens, cotangent, counts, destination, placement, gate_up_weight, down_weight):
@@ -361,9 +371,6 @@
     split = owners // experts
     width, slc = down_weight.shape[1], down_weight.shape[2]
     zs = owners // PAIR
-    fold = max(1, 16 // (2 * tok))
-    cols = width // fold
-    box = fold * 2 * tok
     rows = groups * tok
     per_dot = min(zs, max(1, 64 // rows))
     lanes = -(-2 * rows // 128) * 128
@@ -377,9 +384,12 @@
     vmem = pl.BlockSpec(memory_space=pltpu.VMEM)
     smem = pl.BlockSpec(memory_space=pltpu.SMEM)
     anywhere = pl.BlockSpec(memory_space=pl.ANY)
+    large = zs * rows * width >= (1 << 20)
+    flat = (groups, tok, width) if large else (rows, width)
     shapes = [
         ((groups, 2, tok, width), BF16),
         ((groups, 8, lanes), jnp.int32),
+        ((zs, 8, lanes), jnp.int32),
         ((PAIR, zs, 2, rows, width), BF16),
         ((width, 3 * slc), BF16),
         ((blocks, rows, 2 * slc), BF16),
@@ -388,37 +398,34 @@
         ((groups, share, rows, slc), BF16),
         ((blocks, rows, slc), BF16),
         ((blocks, rows, 2 * slc), BF16),
-        ((zs, 2, rows, width), BF16),
-        ((zs, 2, rows, width), F32 if zs * rows * width < (1 << 20) else BF16),
-        ((zs, 2, rows, width), BF16),
-        ((zs, 2, rows, width), BF16),
-        ((2, rows, width), F32),
-        ((groups, box, cols), BF16),
-        ((groups, box, cols), BF16),
+        ((zs, 2) + flat, BF16),
+        ((zs, 2, rows, width), BF16 if large else F32),
+        ((zs, 2) + flat, BF16),
+        ((1, 1, 1, tok, width) if large else (zs, 2, groups, tok, width), BF16),
+        ((zs, groups, 2, tok, width), BF16),
         ((width, 3 * slc), F32),
     ]
     dma = pltpu.SemaphoreType.DMA
-    out, grads = pl.pallas_call(
-        functools.partial(kernel, (groups, zs, fold, tok, experts, split, per_dot)),
+    out, gate_up_grad, down_grad = pl.pallas_call(
+        functools.partial(kernel, (groups, zs, tok, experts, split, per_dot)),
         out_shape=(
-            jax.ShapeDtypeStruct((groups, box, cols), BF16),
-            jax.ShapeDtypeStruct((3, width, slc), BF16),
+            jax.ShapeDtypeStruct((groups, 2, tok, width) if width % 128 else (2, tok, model), BF16),
+            jax.ShapeDtypeStruct((2, width, slc), BF16),
+            jax.ShapeDtypeStruct((width, slc), BF16),
         ),
         in_specs=[anywhere, anywhere, smem, smem, smem, anywhere, anywhere],
-        out_specs=(vmem, vmem),
+        out_specs=(vmem, vmem, vmem),
         scratch_shapes=[pltpu.VMEM(s, t) for s, t in shapes] + [
-            dma((2, 2 * groups)), dma((2, groups)), dma((2, 2 * zs)), dma((2, 2 * zs)), dma((2, 4 * zs)),
-            dma((2, 2 * groups)), dma((2, 2 * groups)), dma((2, 2 * zs)), dma((2, 2 * zs)), dma((2, groups)),
-            dma((5,)), dma((2,)),
+            dma((2, 2 * groups)), dma((2, groups)), dma((2, zs)), dma((2, 2 * zs)), dma((2, 2 * zs)),
+            dma((2, 2 * groups)), dma((2, 2 * groups)), dma((2, 2 * zs)), dma((2, 2 * zs * groups)), dma((5,)),
         ],
         compiler_params=pltpu.CompilerParams(
             collective_id=0, has_side_effects=True, vmem_limit_bytes=60 << 20
         ),
     )(tokens, cotangent, destination, counts, placement, gate_up_weight[0], down_weight[0])
-    out = out.reshape(groups, fold, 2, tok, cols)
-    out = jnp.transpose(out, (2, 3, 0, 1, 4)).reshape(2, 1, tok, model)
-    grads = grads.astype(F32)
-    return out[0], out[1], grads[None, 0:2], grads[2:3]
+    if width % 128:
+        out = jnp.transpose(out, (1, 2, 0, 3)).reshape(2, tok, model)
+    return out[0:1], out[1:2], gate_up_grad[None].astype(F32), down_grad[None].astype(F32)
 
 
 def solution(mesh):

time: 52.8 us -> 49.2 us (0.932)
  Pallas kernels: 46.5 us -> 43.1 us
  local copies, waits for them, and re-layouts: 4.65 us -> 1.51 us
  other arithmetic: 0.13 us -> 3.11 us
    pallas_call x1, Pallas kernels: 46.5 us -> 43.1 us  [body(): pl.pallas_call(functools.partial(kernel, (groups, zs, tok, experts, split...]
    convert_element_type x1 -> x2, other arithmetic: 0.13 us -> 3.11 us  [the longest x1 2.23 us: body(): gate_up_grad[None].astype(F32)]
    broadcast_in_dim x1 -> x0, local copies, waits for them, and re-layouts: 1.14 us -> none  [body(): return (out[0], out[1], grads[None, 0:2], grads[2:3])]
    slice x2 -> x1, local copies, waits for them, and re-layouts: 2.51 us -> 1.51 us  [body(): out[1:2]]
    reshape x1 -> x0, local copies, waits for them, and re-layouts: 0.99 us -> none  [body(): out = out.reshape(groups, fold, 2, tok, cols)]
where the time goes in v4:
time: 49.2 us; the launch traced here: 49 us
  Pallas kernels  43.1 us (88%)
  other arithmetic  3.11 us (6%)
  local copies, waits for them, and re-layouts  1.51 us (3%)
  between operations  1.3 us (3%)
    pallas_call x1, Pallas kernels, body(): pl.pallas_call(functools.partial(kernel, (groups, zs, tok, experts, split...  43.1 us
    convert_element_type x1, other arithmetic, body(): gate_up_grad[None].astype(F32)  2.23 us
    slice x1, local copies, waits for them, and re-layouts, body(): out[1:2]  1.51 us

profile of v4, /device:TPU:0, one launch (start us, length us, event | category | flops | bytes accessed | tf_op | source)
XLA Modules:
  0.0 49.0 jit_solution(15484531833167522184)
XLA Ops:
  1.3 43.1 %shard_map.102 = (bf16[2,4,5120]{2,1,0:T(4,128)(2,1)}, bf16[2,1280,128]{2,1,0:T(8,128)(2,1)}, bf16[1280,128]{1,0:T(8,128)(2,1)}) custom-call(bf16[1,4,5120]{2,1,0:T(4,128)(2,1)} %tokens_ref.1, bf16[1,4,5120]{2,1,0:T(4,128)(2,1)} %cotangent_ref.1, s32[1,1,4]{2,1,0:T(1,128)} %dest_ref.1, s32[1,1,1]{2,1,0:T(1,128)S(6)} %copy.11.counts_ref, s32[8]{0:T(128)} %placement_ref.1, ...), custom_call_target="tpu_custom_call" | custom-call | tf_op jit(solution)/shard_map/pallas_call | solution.py:409
  44.4 0.0 copy-start
  44.4 1.5 %fusion = (bf16[1,4,5120]{2,1,0:T(4,128)(2,1)}, bf16[1,4,5120]{2,1,0:T(4,128)(2,1)}) fusion(bf16[2,4,5120]{2,1,0:T(4,128)(2,1)} %get-tuple-element.7), kind=kLoop, calls=%fused_computation.2 | loop fusion | bytes 163840 | tf_op jit(solution)/shard_map/slice | solution.py:428
  45.9 2.2 %bitcast_convert_fusion = f32[1,2,1280,128]{3,2,1,0:T(8,128)} fusion(bf16[2,1280,128]{2,1,0:T(8,128)(2,1)} %get-tuple-element.8), kind=kLoop, calls=%fused_computation | loop fusion | flops 327680 | bytes 1966080 | tf_op jit(solution)/shard_map/convert_element_type | solution.py:428
  48.2 0.0 copy-done
  48.2 0.9 %bitcast_convert_fusion.1 = f32[1,1280,128]{2,1,0:T(8,128)} fusion(bf16[1280,128]{1,0:T(8,128)(2,1)S(1)} %copy-done), kind=kLoop, calls=%fused_computation.1 | loop fusion | flops 163840 | bytes 983040 | tf_op jit(solution)/shard_map/convert_element_type | solution.py:428
Async XLA Ops:
  44.4 3.7 %copy-start = (bf16[1280,128]{1,0:T(8,128)(2,1)S(1)}, bf16[1280,128]{1,0:T(8,128)(2,1)}, u32[]{:S(2)}) copy-start(bf16[1280,128]{1,0:T(8,128)(2,1)} %get-tuple-element.9) | copy-start | bytes 983044

commit v5 on v4

--- a/solution.py
+++ b/solution.py
@@ -22,8 +22,8 @@
     dims,
     tokens_ref, cotangent_ref, dest_ref, counts_ref, placement_ref, gate_up_ref, down_ref,
     rows_out, gate_up_out, down_out,
-    inbox, metas, dests, xall, weights, part_gu, part_h, in_gu, in_h, hidden, grads, outrows, mine, yin, placed, zin, acc,
-    pack_sems, meta_sems, dest_sems, z_sems, y_sems, part_sems, grad_sems, yo_sems, zo_sems, w_sems,
+    inbox, metas, xall, weights, turned, part_gu, part_h, in_gu, in_h, hidden, grads, outrows, mine, yin, placed, zin, acc,
+    pack_sems, meta_sems, z_sems, y_sems, part_sems, grad_sems, yo_sems, zo_sems, w_sems,
 ):
     groups, zs, tok, experts, split, per_dot = dims
     if len(outrows.shape) == 5:
@@ -119,7 +119,6 @@
     m_group, m_row = lax.rem(lax.div(m, tok), groups), lax.rem(m, tok)
     slot = slots(m_group, m_row)
     row_at = lax.broadcasted_iota(jnp.int32, (rows, tok), 0)
-    col_at = lax.broadcasted_iota(jnp.int32, (rows, tok), 1)
 
     for copy in meta_copies:
         copy.wait_recv()
@@ -128,11 +127,7 @@
         jnp.where((dest == h) & (lax.rem(slot, cap) < metas[h, 1:2, 0:n_rows]), 1, 0)
         for h in range(groups)
     )
-    dests[z, :, 0:n_rows] = jnp.broadcast_to(dest, (8, n_rows))
-    dest_copies = [remote(dests.at[z], dests.at[z], dest_sems, d, (me, q * PAIR + y)) for d, q in z_peers]
-    for copy in dest_copies:
-        copy.start()
-    sent += dest_copies
+    home = jnp.where(kept > 0, dest * tok + slot, -1)
 
     def own_rows(t):
         loads[t].wait()
@@ -140,8 +135,7 @@
             copy.wait_recv()
         picked = jnp.zeros((rows, width), F32)
         for g in range(groups):
-            keep = kept[:, g * tok:(g + 1) * tok]
-            place = jnp.where((row_at == g * tok + col_at) & (keep > 0), 1.0, 0.0).astype(BF16)
+            place = jnp.where(row_at == home[:, g * tok:(g + 1) * tok], 1.0, 0.0).astype(BF16)
             picked = picked + dot(place, inbox[g, t], (1, 0))
         xall[0, z, t] = picked.astype(BF16)
 
@@ -223,7 +217,7 @@
         if experts == 1:
             return value
         row = lax.broadcasted_iota(jnp.int32, value.shape, 1)
-        expert = lax.div(slots(lax.div(row, tok), lax.rem(row, tok)), cap)
+        expert = lax.div(lax.rem(row, tok), cap)
         return jnp.where(expert == lax.div(placement_ref[ep], split), value, 0.0)
 
     def rows_of(ref, side, first):
@@ -232,7 +226,7 @@
     def produce(side, kind, target):
         def step(first):
             source, low, high = ((hidden, 2, 3), (grads, 0, 2))[kind]
-            out = dot(rows_of(source, side, first), weights[:, low * slc:high * slc], (1, 1))
+            out = dot(rows_of(source, side, first), turned[low * slc:high * slc, :], (1, 0))
             target[pl.ds(first, per_dot), kind] = out.astype(target.dtype).reshape((per_dot,) + target.shape[2:])
 
         each(step)
@@ -251,26 +245,19 @@
             placed.at[q, t, p], zin.at[z, me, t], zo_sems, (t * zs + i) * groups + d, (p, q * PAIR + y)
         )
 
-    slot_at = lax.broadcasted_iota(jnp.int32, (tok, rows), 0)
-
     def send_home(t, copies):
         for i, q in order:
             copies[i].wait()
-            total = (mine[q, t].astype(F32) + yin[q, t].reshape(rows, width).astype(F32)).astype(BF16)
-            going = dests[q, 0:1, 0:rows]
-
-            def place(p):
-                pick = jnp.where((slot_at == slot[:, 0:rows]) & (going == p), 1.0, 0.0).astype(BF16)
-                return dot(pick, total, (1, 0)).astype(BF16)
-
-            def send(d, i=i, q=q, place=place):
-                p = lax.rem(me + d, groups)
-                placed[q, t, p] = place(p)
+            total = mine[q, t].astype(F32) + yin[q, t].reshape(rows, width).astype(F32)
+            for p in range(groups):
+                placed[q, t, p] = total[p * tok:(p + 1) * tok].astype(BF16)
+
+            def send(d, i=i, q=q):
                 deliver(t, i, q, d).start()
 
             for_groups(1 if i == zs - 1 else 0, send)
             if i == zs - 1:
-                zin[z, me, t] = place(me)
+                zin[z, me, t] = placed[q, t, me]
 
     def delivered(t, wait):
         for i, q in order:
@@ -279,9 +266,10 @@
     for t in range(2):
         own_rows(t)
         send_own(t)
-    pass_on(0)
     for load in loads[2:]:
         load.wait()
+    turned[...] = jnp.transpose(weights[...], (1, 0))
+    pass_on(0)
     project(0, 0, 0, 2, part_gu)
     pass_on(1)
     arrivals(0)
@@ -312,8 +300,6 @@
     grads[held, :, slc:2 * slc] = only_served(hidden_grad * activated).astype(BF16)
     grad_copies = share_out(1, grads)
 
-    for copy in dest_copies:
-        copy.wait_recv()
     send_home(0, across_ahead)
 
     for copy in grad_copies:
@@ -383,15 +369,15 @@
     share = blocks // groups
     vmem = pl.BlockSpec(memory_space=pltpu.VMEM)
     smem = pl.BlockSpec(memory_space=pltpu.SMEM)
-    anywhere = pl.BlockSpec(memory_space=pl.ANY)
+    hbm = pl.BlockSpec(memory_space=pltpu.HBM)
     large = zs * rows * width >= (1 << 20)
     flat = (groups, tok, width) if large else (rows, width)
     shapes = [
         ((groups, 2, tok, width), BF16),
         ((groups, 8, lanes), jnp.int32),
-        ((zs, 8, lanes), jnp.int32),
         ((PAIR, zs, 2, rows, width), BF16),
         ((width, 3 * slc), BF16),
+        ((3 * slc, width), BF16),
         ((blocks, rows, 2 * slc), BF16),
         ((blocks, rows, slc), BF16),
         ((groups, share, rows, 2 * slc), BF16),
@@ -413,10 +399,10 @@
             jax.ShapeDtypeStruct((2, width, slc), BF16),
             jax.ShapeDtypeStruct((width, slc), BF16),
         ),
-        in_specs=[anywhere, anywhere, smem, smem, smem, anywhere, anywhere],
+        in_specs=[hbm, hbm, smem, smem, smem, hbm, hbm],
         out_specs=(vmem, vmem, vmem),
         scratch_shapes=[pltpu.VMEM(s, t) for s, t in shapes] + [
-            dma((2, 2 * groups)), dma((2, groups)), dma((2, zs)), dma((2, 2 * zs)), dma((2, 2 * zs)),
+            dma((2, 2 * groups)), dma((2, groups)), dma((2, 2 * zs)), dma((2, 2 * zs)),
             dma((2, 2 * groups)), dma((2, 2 * groups)), dma((2, 2 * zs)), dma((2, 2 * zs * groups)), dma((5,)),
         ],
         compiler_params=pltpu.CompilerParams(

time: 49.2 us -> 48.6 us (0.988)
  Pallas kernels: 43.1 us -> 42.5 us
    pallas_call x1, Pallas kernels: 43.1 us -> 42.5 us  [body(): pl.pallas_call(functools.partial(kernel, (groups, zs, tok, experts, split...]
where the time goes in v5:
time: 48.6 us; the launch traced here: 48.4 us
  Pallas kernels  42.5 us (87%)
  other arithmetic  3.11 us (6%)
  local copies, waits for them, and re-layouts  1.51 us (3%)
  between operations  1.3 us (3%)
    pallas_call x1, Pallas kernels, body(): pl.pallas_call(functools.partial(kernel, (groups, zs, tok, experts, split...  42.5 us
    convert_element_type x1, other arithmetic, body(): gate_up_grad[None].astype(F32)  2.23 us
    slice x1, local copies, waits for them, and re-layouts, body(): out[1:2]  1.51 us

profile of v5, /device:TPU:0, one launch (start us, length us, event | category | flops | bytes accessed | tf_op | source)
XLA Modules:
  0.0 48.4 jit_solution(6374005517684006611)
XLA Ops:
  1.3 42.5 %shard_map.102 = (bf16[2,4,5120]{2,1,0:T(4,128)(2,1)}, bf16[2,1280,128]{2,1,0:T(8,128)(2,1)}, bf16[1280,128]{1,0:T(8,128)(2,1)}) custom-call(bf16[1,4,5120]{2,1,0:T(4,128)(2,1)} %tokens_ref.1, bf16[1,4,5120]{2,1,0:T(4,128)(2,1)} %cotangent_ref.1, s32[1,1,4]{2,1,0:T(1,128)} %dest_ref.1, s32[1,1,1]{2,1,0:T(1,128)S(6)} %copy.11.counts_ref, s32[8]{0:T(128)} %placement_ref.1, ...), custom_call_target="tpu_custom_call" | custom-call | tf_op jit(solution)/shard_map/pallas_call | solution.py:395
  43.8 0.0 copy-start
  43.8 1.5 %fusion = (bf16[1,4,5120]{2,1,0:T(4,128)(2,1)}, bf16[1,4,5120]{2,1,0:T(4,128)(2,1)}) fusion(bf16[2,4,5120]{2,1,0:T(4,128)(2,1)} %get-tuple-element.7), kind=kLoop, calls=%fused_computation.2 | loop fusion | bytes 163840 | tf_op jit(solution)/shard_map/slice | solution.py:414
  45.3 2.2 %bitcast_convert_fusion = f32[1,2,1280,128]{3,2,1,0:T(8,128)} fusion(bf16[2,1280,128]{2,1,0:T(8,128)(2,1)} %get-tuple-element.8), kind=kLoop, calls=%fused_computation | loop fusion | flops 327680 | bytes 1966080 | tf_op jit(solution)/shard_map/convert_element_type | solution.py:414
  47.5 0.0 copy-done
  47.5 0.9 %bitcast_convert_fusion.1 = f32[1,1280,128]{2,1,0:T(8,128)} fusion(bf16[1280,128]{1,0:T(8,128)(2,1)S(1)} %copy-done), kind=kLoop, calls=%fused_computation.1 | loop fusion | flops 163840 | bytes 983040 | tf_op jit(solution)/shard_map/convert_element_type | solution.py:414
Async XLA Ops:
  43.8 3.7 %copy-start = (bf16[1280,128]{1,0:T(8,128)(2,1)S(1)}, bf16[1280,128]{1,0:T(8,128)(2,1)}, u32[]{:S(2)}) copy-start(bf16[1280,128]{1,0:T(8,128)(2,1)} %get-tuple-element.9) | copy-start | bytes 983044

commit v6 on v5

--- a/solution.py
+++ b/solution.py
@@ -22,8 +22,8 @@
     dims,
     tokens_ref, cotangent_ref, dest_ref, counts_ref, placement_ref, gate_up_ref, down_ref,
     rows_out, gate_up_out, down_out,
-    inbox, metas, xall, weights, turned, part_gu, part_h, in_gu, in_h, hidden, grads, outrows, mine, yin, placed, zin, acc,
-    pack_sems, meta_sems, z_sems, y_sems, part_sems, grad_sems, yo_sems, zo_sems, w_sems,
+    inbox, metas, xall, weights, turned, part_gu, part_h, in_gu, in_h, hidden, grads, outrows, mine, yin, placed, zin, acc, gate_up_held, down_held,
+    pack_sems, meta_sems, z_sems, y_sems, part_sems, grad_sems, yo_sems, zo_sems, w_sems, o_sems,
 ):
     groups, zs, tok, experts, split, per_dot = dims
     if len(outrows.shape) == 5:
@@ -307,28 +307,34 @@
     produce(1, 1, outrows)
     across_back = send_across(1)
     produce(0, 1, mine)
-    send_home(1, across_back)
-
-    if blocks == PAIR * per_dot:
-        def both_sides(ref):
-            return ref[...].reshape(blocks * rows, ref.shape[-1])
-
-        def all_rows(kind):
-            return xall[:, :, kind].reshape(blocks * rows, width)
-
-        acc[:, 0:2 * slc] = dot(all_rows(0), both_sides(grads), (0, 0))
-        acc[:, 2 * slc:3 * slc] = dot(all_rows(1), both_sides(hidden), (0, 0))
-    else:
-        acc[...] = jnp.zeros_like(acc)
+
+    def weight_grad(kind, ref, low, high):
+        at = slice(low * slc, high * slc)
+        if blocks == PAIR * per_dot:
+            acc[:, at] = dot(
+                xall[:, :, kind].reshape(blocks * rows, width),
+                ref[...].reshape(blocks * rows, ref.shape[-1]), (0, 0),
+            )
+            return
+        acc[:, at] = jnp.zeros((width, (high - low) * slc), F32)
         for side in range(PAIR):
             def step(first, side=side):
-                acc[:, 0:2 * slc] += dot(x_rows(side, first, 0), rows_of(grads, side, first), (0, 0))
-                acc[:, 2 * slc:3 * slc] += dot(x_rows(side, first, 1), rows_of(hidden, side, first), (0, 0))
+                acc[:, at] += dot(x_rows(side, first, kind), rows_of(ref, side, first), (0, 0))
 
             each(step)
+
+    weight_grad(1, hidden, 2, 3)
+    down_held[...] = acc[:, 2 * slc:3 * slc].astype(down_held.dtype)
+    stores = [
+        pltpu.make_async_copy(down_held, down_out, o_sems.at[0]),
+        pltpu.make_async_copy(gate_up_held, gate_up_out, o_sems.at[1]),
+    ]
+    stores[0].start()
+    send_home(1, across_back)
+    weight_grad(0, grads, 0, 2)
     for i in range(2):
-        gate_up_out[i] = acc[:, i * slc:(i + 1) * slc].astype(gate_up_out.dtype)
-    down_out[...] = acc[:, 2 * slc:3 * slc].astype(down_out.dtype)
+        gate_up_held[i] = acc[:, i * slc:(i + 1) * slc].astype(gate_up_held.dtype)
+    stores[1].start()
 
     for t in range(2):
         delivered(t, lambda copy: copy.wait_recv())
@@ -342,6 +348,8 @@
             else:
                 rows_out[g, t] = total
     sent += gu_copies + h_copies + hidden_copies + grad_copies
+    for store in stores:
+        store.wait()
     for copy in sent:
         copy.wait_send()
     for t in range(2):
@@ -390,6 +398,8 @@
         ((1, 1, 1, tok, width) if large else (zs, 2, groups, tok, width), BF16),
         ((zs, groups, 2, tok, width), BF16),
         ((width, 3 * slc), F32),
+        ((2, width, slc), BF16),
+        ((width, slc), BF16),
     ]
     dma = pltpu.SemaphoreType.DMA
     out, gate_up_grad, down_grad = pl.pallas_call(
@@ -400,10 +410,10 @@
             jax.ShapeDtypeStruct((width, slc), BF16),
         ),
         in_specs=[hbm, hbm, smem, smem, smem, hbm, hbm],
-        out_specs=(vmem, vmem, vmem),
+        out_specs=(vmem, hbm, hbm),
         scratch_shapes=[pltpu.VMEM(s, t) for s, t in shapes] + [
             dma((2, 2 * groups)), dma((2, groups)), dma((2, 2 * zs)), dma((2, 2 * zs)),
-            dma((2, 2 * groups)), dma((2, 2 * groups)), dma((2, 2 * zs)), dma((2, 2 * zs * groups)), dma((5,)),
+            dma((2, 2 * groups)), dma((2, 2 * groups)), dma((2, 2 * zs)), dma((2, 2 * zs * groups)), dma((5,)), dma((2,)),
         ],
         compiler_params=pltpu.CompilerParams(
             collective_id=0, has_side_effects=True, vmem_limit_bytes=60 << 20

time: 48.6 us -> 48.3 us (level)
  no operation moved by 1% of the time
where the time goes in v6:
time: 48.3 us; the launch traced here: 48.1 us
  Pallas kernels  42.2 us (87%)
  other arithmetic  3.11 us (6%)
  local copies, waits for them, and re-layouts  1.51 us (3%)
  between operations  1.3 us (3%)
    pallas_call x1, Pallas kernels, body(): pl.pallas_call(functools.partial(kernel, (groups, zs, tok, experts, split...  42.2 us
    convert_element_type x1, other arithmetic, body(): gate_up_grad[None].astype(F32)  2.23 us
    slice x1, local copies, waits for them, and re-layouts, body(): out[1:2]  1.51 us

profile of v6, /device:TPU:0, one launch (start us, length us, event | category | flops | bytes accessed | tf_op | source)
XLA Modules:
  0.0 48.1 jit_solution(4724062023278135)
XLA Ops:
  1.3 42.2 %shard_map.102 = (bf16[2,4,5120]{2,1,0:T(4,128)(2,1)}, bf16[2,1280,128]{2,1,0:T(8,128)(2,1)}, bf16[1280,128]{1,0:T(8,128)(2,1)}) custom-call(bf16[1,4,5120]{2,1,0:T(4,128)(2,1)} %tokens_ref.1, bf16[1,4,5120]{2,1,0:T(4,128)(2,1)} %cotangent_ref.1, s32[1,1,4]{2,1,0:T(1,128)} %dest_ref.1, s32[1,1,1]{2,1,0:T(1,128)S(6)} %copy.11.counts_ref, s32[8]{0:T(128)} %placement_ref.1, ...), custom_call_target="tpu_custom_call" | custom-call | tf_op jit(solution)/shard_map/pallas_call | solution.py:405
  43.5 0.0 copy-start
  43.5 1.5 %fusion = (bf16[1,4,5120]{2,1,0:T(4,128)(2,1)}, bf16[1,4,5120]{2,1,0:T(4,128)(2,1)}) fusion(bf16[2,4,5120]{2,1,0:T(4,128)(2,1)} %get-tuple-element.7), kind=kLoop, calls=%fused_computation.2 | loop fusion | bytes 163840 | tf_op jit(solution)/shard_map/slice | solution.py:424
  45.0 2.2 %bitcast_convert_fusion = f32[1,2,1280,128]{3,2,1,0:T(8,128)} fusion(bf16[2,1280,128]{2,1,0:T(8,128)(2,1)} %get-tuple-element.8), kind=kLoop, calls=%fused_computation | loop fusion | flops 327680 | bytes 1966080 | tf_op jit(solution)/shard_map/convert_element_type | solution.py:424
  47.2 0.0 copy-done
  47.2 0.9 %bitcast_convert_fusion.1 = f32[1,1280,128]{2,1,0:T(8,128)} fusion(bf16[1280,128]{1,0:T(8,128)(2,1)S(1)} %copy-done), kind=kLoop, calls=%fused_computation.1 | loop fusion | flops 163840 | bytes 983040 | tf_op jit(solution)/shard_map/convert_element_type | solution.py:424
Async XLA Ops:
  43.5 3.7 %copy-start = (bf16[1280,128]{1,0:T(8,128)(2,1)S(1)}, bf16[1280,128]{1,0:T(8,128)(2,1)}, u32[]{:S(2)}) copy-start(bf16[1280,128]{1,0:T(8,128)(2,1)} %get-tuple-element.9) | copy-start | bytes 983044
